TPU v7x, 32 devices: a whole 2x2x4 slice. The times are simulated.
32 devices in a mesh: tile: 16 (over z, y, core), pgroup: 2 (over x).
Axes of the slice: x: 2, y: 2, z: 4, core: 2. Of those that a mesh axis runs over, the one named last changes fastest.
Arguments:
- echoes: bfloat16 [2048, 2, 4096], P(('pgroup', 'tile')), may hold values from -6 to 6
- offsets: int32 [16, 2048], P('tile', 'pgroup'), may hold values from 0 to 3577
- phase_index: int32 [16, 2048], P('tile', 'pgroup'), may hold values from 0 to 15
- steering: float32 [2, 16, 2048], P(None, 'tile'), may hold values from -2 to 2
- kernels: float32 [16, 8], replicated, may hold values from -2 to 2
Outputs:
- image: float32 [2, 512, 4096], P(None, 'pgroup', 'tile')
All inputs are finite; a program needn't handle non-finite values.
Results may differ from a plain program's by a relative error of at most 0.0037.
Values may be sent and summed in bfloat16 or wider, within the bound.
No kernel may reach another device: no remote copies, remote signals or barrier semaphores. Data moves between devices by JAX's collectives and lax.ppermute only.
A program may use at most 64 MiB of HBM per device.

v0:
```python
import jax
import jax.numpy as jnp
from jax import lax
from jax.sharding import PartitionSpec as P

ROW_DEV = 256
COL_DEV = 256
STEPS = 4


def passed_along(shard, axis, by):
    length = lax.axis_size(axis)
    return lax.ppermute(shard, axis, [(i, (i + by) % length) for i in range(length)])


def steer_table(rates, curves, columns):
    centred = jnp.arange(columns, dtype=jnp.float32) - (columns - 1) / 2.0
    angle = (
        rates[:, None] * centred[None, :] + curves[:, None] * (centred * centred / columns)[None, :]
    )
    return (jnp.cos(angle).astype(jnp.bfloat16), jnp.sin(angle).astype(jnp.bfloat16))


def shifted_window(pulse_rows, firsts, span):
    length = pulse_rows.shape[2]
    bit_count = max(1, (length - span).bit_length())
    padded_len = span + (1 << bit_count) - 1
    current = jnp.pad(pulse_rows, ((0, 0), (0, 0), (0, max(0, padded_len - length))))
    for level in range(bit_count - 1, -1, -1):
        step_len = 1 << level
        keep = span + step_len - 1
        chosen = (firsts // step_len % 2 == 1)[:, None, None]
        current = jnp.where(chosen, current[:, :, step_len : step_len + keep], current[:, :, :keep])
    return current


def build_profile(pulse_rows, firsts, phases, kernels, row_count):
    taps = kernels.shape[1]
    span = row_count + taps - 1
    window = shifted_window(pulse_rows, firsts, span)
    onehot = (phases[:, None] == jnp.arange(kernels.shape[0], dtype=jnp.int32)[None, :]).astype(
        jnp.float32
    )
    weights = jnp.dot(onehot, kernels, precision=lax.Precision.HIGHEST)
    summed_taps = jnp.zeros((pulse_rows.shape[0], 2, row_count), jnp.float32)
    for tap_index in range(taps):
        summed_taps = summed_taps + weights[:, tap_index, None, None] * window[
            :, :, tap_index : tap_index + row_count
        ].astype(jnp.float32)
    return summed_taps.astype(jnp.bfloat16)


def contract(left, right):
    return lax.dot_general(
        left, right, (((0,), (0,)), ((), ())), preferred_element_type=jnp.float32
    )


def project(profile, cosine, sine):
    real_part = contract(profile[:, 0], cosine) - contract(profile[:, 1], sine)
    imag_part = contract(profile[:, 0], sine) + contract(profile[:, 1], cosine)
    return jnp.stack([real_part, imag_part])


def per_device(echoes, offsets, phase_index, steering, kernels):
    pulse_dev = echoes.shape[0]
    tile_count = lax.axis_size("tile")
    group_count = lax.axis_size("pgroup")
    row_count = ROW_DEV * group_count
    columns = COL_DEV
    tile_index = lax.axis_index("tile")
    group_index = lax.axis_index("pgroup")
    delays = offsets[0]
    phase_rows = phase_index[0]
    rates = steering[0, 0]
    curves = steering[1, 0]
    normaliser = (STEPS * pulse_dev * group_count) ** (-0.5)
    local_starts = [(tile_index - distance) % tile_count * pulse_dev for distance in range(STEPS)]
    profiles = []
    blocks = [echoes]
    current = echoes
    for distance in range(1, STEPS):
        current = passed_along(current, "tile", 1)
        blocks.append(current)
    for distance in range(STEPS):
        first = local_starts[distance]
        firsts = lax.dynamic_slice_in_dim(delays, first, pulse_dev)
        phases = lax.dynamic_slice_in_dim(phase_rows, first, pulse_dev)
        profiles.append(build_profile(blocks[distance], firsts, phases, kernels, row_count))
    partial_value = jnp.zeros((2, row_count, columns), jnp.float32)
    for distance in range(STEPS):
        global_first = group_index * tile_count * pulse_dev + local_starts[distance]
        cosine, sine = steer_table(
            lax.dynamic_slice_in_dim(rates, global_first, pulse_dev),
            lax.dynamic_slice_in_dim(curves, global_first, pulse_dev),
            columns,
        )
        partial_value = partial_value + project(profiles[distance], cosine, sine)
    summed = lax.psum_scatter(partial_value, "pgroup", scatter_dimension=1, tiled=True)
    return summed * normaliser


def solution(mesh):
    placed = (
        P(("pgroup", "tile"), None, None),
        P("tile", "pgroup"),
        P("tile", "pgroup"),
        P(None, "tile", None),
        P(),
    )
    return jax.shard_map(
        per_device, mesh=mesh, in_specs=placed, out_specs=P(None, "pgroup", "tile"), check_vma=False
    )
```

profile of v0, /device:TPU:0, one launch (start us, length us, event | category | flops | bytes accessed | tf_op | source)
XLA Modules:
  0.0 99.6 jit_solution(16397204672318506099)
XLA Ops:
  6.6 1.8 %copy.6 = bf16[64,2,4096]{2,0,1:T(8,128)(2,1)S(1)} copy(bf16[64,2,4096]{2,1,0:T(2,128)(2,1)} %param.5) | data formatting | bytes 2097152 | tf_op args[0]
  8.4 0.5 collective-permute-start
  10.4 0.2 fusion.10
  12.0 14.4 %collective-permute-done = bf16[64,2,4096]{2,0,1:T(8,128)(2,1)S(1)} collective-permute-done((bf16[64,2,4096]{2,0,1:T(8,128)(2,1)S(1)}, bf16[64,2,4096]{2,0,1:T(8,128)(2,1)S(1)}, u32[]{:S(2)}, u32[]{:S(2)}) %collective-permute-start) | collective-permute-done | bytes 1048608 | tf_op jit(solution)/shard_map/ppermute | solution.py:13
  26.4 0.2 fusion.11
  28.0 0.4 add_convert_fusion.3
  28.5 0.5 fusion.14
  29.0 0.5 fusion.15
  29.5 0.5 fusion.6
  30.0 0.5 fusion.7
  30.5 0.4 add_convert_fusion.2
  31.0 0.5 fusion.16
  31.5 0.5 fusion.4
  32.0 0.5 fusion.17
  32.5 0.5 fusion.5
  33.0 14.0 %collective-permute-done.1 = bf16[64,2,4096]{2,0,1:T(8,128)(2,1)S(1)} collective-permute-done((bf16[64,2,4096]{2,0,1:T(8,128)(2,1)S(1)}, bf16[64,2,4096]{2,0,1:T(8,128)(2,1)S(1)}, u32[]{:S(2)}, u32[]{:S(2)}) %collective-permute-start.1) | collective-permute-done | bytes 1048608 | tf_op jit(solution)/shard_map/ppermute | solution.py:13
  46.9 0.2 fusion.12
  47.7 0.2 collective-permute-start.2
  48.6 16.3 %collective-permute-done.2 = bf16[64,2,4096]{2,0,1:T(8,128)(2,1)S(1)} collective-permute-done((bf16[64,2,4096]{2,0,1:T(8,128)(2,1)S(1)}, bf16[64,2,4096]{2,0,1:T(8,128)(2,1)S(1)}, u32[]{:S(2)}, u32[]{:S(2)}) %collective-permute-start.2) | collective-permute-done | bytes 1048608 | tf_op jit(solution)/shard_map/ppermute | solution.py:13
  66.5 0.4 add_convert_fusion.1
  67.0 0.5 fusion.18
  67.5 0.5 fusion.19
  68.0 0.4 add_convert_fusion
  68.4 0.5 fusion.20
  68.9 0.5 fusion.21
  69.4 0.5 fusion.2
  69.9 0.5 fusion.3
  70.4 0.5 fusion
  70.9 0.5 fusion.1
  71.4 1.3 %fusion.9 = f32[2,512,256]{2,1,0:T(8,128)} fusion(f32[1,512,256]{2,1,0:T(8,128)S(1)} %fusion.6, f32[1,512,256]{2,1,0:T(8,128)S(1)} %fusion.7, f32[1,512,256]{2,1,0:T(8,128)S(1)} %fusion.4, f32[1,512,256]{2,1,0:T(8,128)S(1)} %fusion.5, f32[1,512,256]{2,1,0:T(8,128)S(1)} %fusion.2, f32[1,512,256]{2,1,0:T(8,128)S(1)} %fusion.3, f32[1,512,256]{2,1,0:T(8,128)S(1)} %fusion, ...), kind=kLoop, calls=%fused_computation.22 | loop fusion | flops 1835008 | bytes 5242880 | tf_op jit(solution)/shard_map/add | solution.py:98
  72.7 18.2 %reduce-scatter.2.cloned.1.call-done = f32[2,256,256]{2,1,0:T(8,128)} async-done(((f32[2,512,256]{2,1,0:T(8,128)}), f32[2,256,256]{2,1,0:T(8,128)}) %reduce-scatter.2.cloned.1.call-update) | async-done | bytes 524304 | tf_op jit(solution)/shard_map/reduce_scatter | solution.py:99
  90.8 1.9 %broadcast_multiply_fusion = f32[2,256,256]{2,1,0:T(8,128)} fusion(f32[2,256,256]{2,1,0:T(8,128)} %reduce-scatter.2.cloned.1.call-done), kind=kLoop, calls=%fused_computation.35 | loop fusion | flops 131072 | bytes 1048576 | tf_op jit(solution)/shard_map/mul | solution.py:100
  (72 shorter events, 6.7 us)
Async XLA Ops:
  6.5 2.5 %copy-start = (f32[16,8]{0,1:T(8,128)S(1)}, f32[16,8]{0,1:T(8,128)}, u32[]{:S(2)}) copy-start(f32[16,8]{0,1:T(8,128)} %param.9) | copy-start | bytes 1540
  6.5 2.4 %copy-start.3 = (s32[1,1024]{1,0:T(1,128)S(1)}, s32[1,1024]{1,0:T(1,128)}, u32[]{:S(2)}) copy-start(s32[1,1024]{1,0:T(1,128)} %param.7) | copy-start | bytes 12292
  6.5 3.4 %copy-start.2 = (s32[1,1024]{1,0:T(1,128)S(1)}, s32[1,1024]{1,0:T(1,128)}, u32[]{:S(2)}) copy-start(s32[1,1024]{1,0:T(1,128)} %param.6) | copy-start | bytes 12292
  6.5 3.8 %copy-start.1 = (f32[2,1,2048]{2,1,0:T(1,128)S(1)}, f32[2,1,2048]{2,1,0:T(1,128)}, u32[]{:S(2)}) copy-start(f32[2,1,2048]{2,1,0:T(1,128)} %param.8) | copy-start | bytes 49156
  6.5 84.3 %reduce-scatter.2.cloned.1.call-start = ((), (), s32[]{:S(2)}) async-start(), calls=%async_computation.1 | async-start | bytes 1572864 | tf_op jit(solution)/shard_map/reduce_scatter | solution.py:99
  8.4 18.0 %collective-permute-start = (bf16[64,2,4096]{2,0,1:T(8,128)(2,1)S(1)}, bf16[64,2,4096]{2,0,1:T(8,128)(2,1)S(1)}, u32[]{:S(2)}, u32[]{:S(2)}) collective-permute-start(bf16[64,2,4096]{2,0,1:T(8,128)(2,1)S(1)} %copy.6), channel_id=1, source_target_pairs={{0,2},{2,4},{4,6},{6,8},{8,10},{10,12},{12,14},{14,16},{16,18},{18... | collective-permute-start | bytes 3145736 | tf_op jit(solution)/shard_map/ppermute | solution.py:13
  30.0 17.0 %collective-permute-start.1 = (bf16[64,2,4096]{2,0,1:T(8,128)(2,1)S(1)}, bf16[64,2,4096]{2,0,1:T(8,128)(2,1)S(1)}, u32[]{:S(2)}, u32[]{:S(2)}) collective-permute-start(bf16[64,2,4096]{2,0,1:T(8,128)(2,1)S(1)} %collective-permute-done), channel_id=1, source_target_pairs={{0,2},{2,4},{4,6},{6,8},{8,10},{10,12},{12,14},{14,16},{16,18},{18... | collective-permute-start | bytes 3145736 | tf_op jit(solution)/shard_map/ppermute | solution.py:13
  47.7 17.2 %collective-permute-start.2 = (bf16[64,2,4096]{2,0,1:T(8,128)(2,1)S(1)}, bf16[64,2,4096]{2,0,1:T(8,128)(2,1)S(1)}, u32[]{:S(2)}, u32[]{:S(2)}) collective-permute-start(bf16[64,2,4096]{2,0,1:T(8,128)(2,1)S(1)} %collective-permute-done.1), channel_id=1, source_target_pairs={{0,2},{2,4},{4,6},{6,8},{8,10},{10,12},{12,14},{14,16},{16,18},{18... | collective-permute-start | bytes 3145736 | tf_op jit(solution)/shard_map/ppermute | solution.py:13
Sparse Core Ops, SparseCore 0:
  72.8 17.9 reduce-scatter.1
where the time goes:
time: 99.7 us; the launch traced here: 99.6 us
  waiting for transfers between devices  62.8 us (63%)
  between operations  14 us (14%)
  other arithmetic  11.2 us (11%)
  matrix products  8.66 us (9%)
  local copies, waits for them, and re-layouts  2.05 us (2%)
    ppermute x3, waiting for transfers between devices, passed_along(): lax.ppermute(shard, axis, [(i, (i + by) % length) for i in range(length)])  44.7 us
    reduce_scatter x1, waiting for transfers between devices, per_device(): lax.psum_scatter(partial_value, 'pgroup', scatter_dimension=1, tiled=True)  18.2 us
    dot_general x16, matrix products, contract(): lax.dot_general(left, right, (((0,), (0,)), ((), ())), preferred_element_...  7.87 us
    select_n x46, other arithmetic, shifted_window(): jnp.where(chosen, current[:, :, step_len:step_len + keep], current[:, :,...  5.88 us
  transfers between devices with their start and end apart: 4, of which 4 were waited for; matrix products, arithmetic and copies ran while one was open for 6% of the time, Pallas kernels for 0%

commit v1 on v0

v1 whole, which is shorter than its diff:
```python
import functools
import math

import jax
import jax.numpy as jnp
import numpy as np
from jax import lax
from jax.experimental import pallas as pl
from jax.experimental.pallas import tpu as pltpu
from jax.sharding import PartitionSpec as P

ROW_DEV = 256
COL_DEV = 256
STEPS = 4
LANES = 128


def fitted(function, terms):
    nodes = np.cos(np.pi * (np.arange(64) + 0.5) / 64) * 0.25 + 0.25
    values = function(nodes)
    scale = np.vander(nodes * nodes, terms, increasing=True)
    return [float(c) for c in np.linalg.lstsq(scale, values, rcond=None)[0]]


COSINE = fitted(lambda x: np.cos(2 * np.pi * x), 9)
SINE = fitted(lambda x: np.sin(2 * np.pi * x) / x, 8)


def horner(coefficients, z):
    total = jnp.full_like(z, coefficients[-1])
    for c in coefficients[-2::-1]:
        total = total * z + c
    return total


def whole(space=pltpu.VMEM):
    return pl.BlockSpec(memory_space=space)


def table_kernel(count, pulse_dev, steer_ref, table_ref):
    columns = COL_DEV
    u = lax.broadcasted_iota(jnp.int32, (1, columns), 1).astype(jnp.float32)
    centred = u - (columns - 1) / 2.0
    linear = centred * (1.0 / (2 * math.pi))
    square = centred * centred * (1.0 / (2 * math.pi * columns))
    for s in range(count):
        rates = steer_ref[pl.ds(s * pulse_dev, pulse_dev), 0:1]
        curves = steer_ref[pl.ds(s * pulse_dev, pulse_dev), 1:2]
        turns = rates * linear + curves * square
        x = turns - jnp.round(turns)
        z = x * x
        cosine = horner(COSINE, z)
        sine = horner(SINE, z) * x
        c16 = cosine.astype(jnp.bfloat16)
        s16 = sine.astype(jnp.bfloat16)
        m16 = (-sine).astype(jnp.bfloat16)
        at = 2 * s * pulse_dev
        table_ref[at : at + pulse_dev, :columns] = c16
        table_ref[at : at + pulse_dev, columns:] = s16
        table_ref[at + pulse_dev : at + 2 * pulse_dev, :columns] = m16
        table_ref[at + pulse_dev : at + 2 * pulse_dev, columns:] = c16


def profile_kernel(pulse_dev, rows, range_rows, taps, groups, count, where_ref, group_ref, kern_ref, echo_ref, *rest):
    outs, scratch = rest[:-1], rest[-1]
    tall = 2 * rows // LANES
    lane = lax.broadcasted_iota(jnp.int32, (tall, LANES), 1)
    top = 2 * (range_rows - rows // LANES)
    me = group_ref[0]

    for i in range(count):

        def one(p, carry, i=i):
            first = where_ref[i, 0, p]
            phase = where_ref[i, 1, p]
            a = lax.shift_right_logical(first, 7) * 2
            b = jnp.bitwise_and(first, LANES - 1)
            x0 = echo_ref[p, pl.ds(a, tall), :]
            x1 = echo_ref[p, pl.ds(a + 2, tall), :]
            x2 = echo_ref[p, pl.ds(jnp.minimum(a + 4, top), tall), :]
            keep = lane >= b
            turn = LANES - b
            w0 = pltpu.roll(jnp.where(keep, x0, x1), turn, 1)
            w1 = pltpu.roll(jnp.where(keep, x1, x2), turn, 1)
            total = kern_ref[phase, 0] * w0
            for j in range(1, taps):
                shifted = pltpu.roll(jnp.where(lane >= j, w0, w1), LANES - j, 1)
                total = total + kern_ref[phase, j] * shifted
            scratch[pl.ds(p * tall, tall), :] = total
            return carry

        lax.fori_loop(0, pulse_dev, one, 0, unroll=8)
        for f in range(groups):
            half = lax.rem(me + f, groups)
            per = ROW_DEV // LANES
            for r in range(per):
                parts = [scratch[pl.ds(half * (2 * per) + 2 * r + q, pulse_dev, stride=tall), :] for q in range(2)]
                both = jnp.concatenate(parts, axis=0)
                outs[i * groups + f][r * LANES : (r + 1) * LANES, :] = both.T.astype(jnp.bfloat16)


def project_kernel(count, normaliser, *refs):
    table_ref, out_ref = refs[count], refs[count + 1]
    left = jnp.concatenate([r[...] for r in refs[:count]], axis=1)
    image = jnp.dot(left, table_ref[...], preferred_element_type=jnp.float32)
    out_ref[0] = image[:, :COL_DEV] * normaliser
    out_ref[1] = image[:, COL_DEV:] * normaliser


def per_device(tile_count, group_count, echoes, offsets, phase_index, steering, kernels):
    pulse_dev, _, length = echoes.shape
    taps = kernels.shape[1]
    rows = ROW_DEV * group_count
    range_rows = length // LANES
    tile = lax.axis_index("tile")
    group = lax.axis_index("pgroup")
    normaliser = (STEPS * pulse_dev * group_count) ** (-0.5)

    def sent(x, by, flip):
        pairs = []
        for t in range(tile_count):
            for g in range(group_count):
                to = ((t + by) % tile_count) * group_count + (g + flip) % group_count
                pairs.append((t * group_count + g, to))
        return lax.ppermute(x, ("tile", "pgroup"), pairs)

    def where(distance):
        first = (tile - distance) % tile_count * pulse_dev
        pair = jnp.concatenate([offsets, phase_index], axis=0)
        return lax.dynamic_slice_in_dim(pair, first, pulse_dev, 1)

    asked = [sent(where(d), -d, 0) for d in range(1, STEPS)]
    spread = echoes.reshape(pulse_dev, 2, range_rows, LANES).transpose(0, 2, 1, 3).astype(jnp.float32)
    spread = spread.reshape(pulse_dev, 2 * range_rows, LANES)
    me = group.reshape(1)

    def profiles(wheres):
        count = wheres.shape[0]
        shape = jax.ShapeDtypeStruct((ROW_DEV, 2 * pulse_dev), jnp.bfloat16)
        return pl.pallas_call(
            functools.partial(profile_kernel, pulse_dev, rows, range_rows, taps, group_count, count),
            out_shape=[shape] * (count * group_count),
            in_specs=[whole(pltpu.SMEM), whole(pltpu.SMEM), whole(pltpu.SMEM), whole()],
            out_specs=[whole()] * (count * group_count),
            scratch_shapes=[pltpu.VMEM((pulse_dev * 2 * rows // LANES, LANES), jnp.float32)],
            compiler_params=pltpu.CompilerParams(vmem_limit_bytes=24 * 1024 * 1024),
            name="profiles",
        )(wheres, me, kernels, spread)

    own = profiles(where(0)[None])
    arrived = [[own[0]] + [sent(own[f], 0, f) for f in range(1, group_count)]]

    count = STEPS * group_count
    steer = steering[:, 0].reshape(2, group_count, tile_count, pulse_dev)
    picked = []
    for d in range(STEPS):
        for f in range(group_count):
            at = ((group - f) % group_count, (tile - d) % tile_count)
            piece = lax.dynamic_slice(steer, (0, at[0], at[1], 0), (2, 1, 1, pulse_dev))
            picked.append(piece.reshape(2, pulse_dev))
    picked = jnp.concatenate(picked, axis=1).T
    table = pl.pallas_call(
        functools.partial(table_kernel, count, pulse_dev),
        out_shape=jax.ShapeDtypeStruct((2 * count * pulse_dev, 2 * COL_DEV), jnp.bfloat16),
        in_specs=[whole()],
        out_specs=whole(),
        compiler_params=pltpu.CompilerParams(vmem_limit_bytes=24 * 1024 * 1024),
        name="steering_table",
    )(picked)

    far = profiles(jnp.stack(asked))
    for d in range(1, STEPS):
        arrived.append([sent(far[(d - 1) * group_count + f], d, f) for f in range(group_count)])

    left = [arrived[d][f] for d in range(STEPS) for f in range(group_count)]
    return pl.pallas_call(
        functools.partial(project_kernel, count, normaliser),
        out_shape=jax.ShapeDtypeStruct((2, ROW_DEV, COL_DEV), jnp.float32),
        in_specs=[whole()] * (count + 1),
        out_specs=whole(),
        compiler_params=pltpu.CompilerParams(vmem_limit_bytes=24 * 1024 * 1024),
        name="project",
    )(*left, table)


def solution(mesh):
    placed = (
        P(("pgroup", "tile"), None, None),
        P("tile", "pgroup"),
        P("tile", "pgroup"),
        P(None, "tile", None),
        P(),
    )
    body = functools.partial(per_device, mesh.shape["tile"], mesh.shape["pgroup"])
    return jax.shard_map(body, mesh=mesh, in_specs=placed, out_specs=P(None, "pgroup", "tile"), check_vma=False)
```

time: 99.7 us -> 35.3 us (0.35)
  waiting for transfers between devices: 62.8 us -> 7.31 us
  between operations: 14 us -> 0.15 us
  starting transfers between devices: 0.83 us -> 13.2 us
  Pallas kernels: 0 us -> 10.9 us
  matrix products: 8.66 us -> 0 us
  other arithmetic: 11.2 us -> 2.99 us
  local copies, waits for them, and re-layouts: 2.05 us -> 0.43 us
    ppermute x3 -> x10, waiting for transfers between devices: 44.7 us -> 7.31 us  [sent(): return lax.ppermute(x, ('tile', 'pgroup'), pairs)]
    reduce_scatter x1 -> x0, waiting for transfers between devices: 18.2 us -> none  [per_device(): lax.psum_scatter(partial_value, 'pgroup', scatter_dimension=1, tiled=True)]
    ppermute x3 -> x10, starting transfers between devices: 0.8 us -> 13.2 us  [sent(): return lax.ppermute(x, ('tile', 'pgroup'), pairs)]
    pallas_call x0 -> x4, Pallas kernels: none -> 10.9 us  [the longest x2 8.85 us: profiles(): pl.pallas_call(functools.partial(profile_kernel, pulse_dev, rows, range_r...]
    dot_general x20 -> x0, matrix products: 8.66 us -> none  [the longest x16 7.87 us: contract(): lax.dot_general(left, right, (((0,), (0,)), ((), ())), preferred_element_...]
    select_n x46 -> x0, other arithmetic: 5.88 us -> none  [shifted_window(): jnp.where(chosen, current[:, :, step_len:step_len + keep], current[:, :,...]
    reshape x0 -> x1, other arithmetic: none -> 2.08 us  [per_device(): spread = spread.reshape(pulse_dev, 2 * range_rows, LANES)]
    mul x1 -> x0, other arithmetic: 1.88 us -> none  [per_device(): return summed * normaliser]
  transfers between devices with their start and end apart: 4 -> 10, of which waited for: 4 -> 5; matrix products, arithmetic and copies ran while one was open for 6% -> 7% of each run, Pallas kernels for 0% -> 28%
where the time goes in v1:
time: 35.3 us; the launch traced here: 34.9 us
  starting transfers between devices  13.2 us (37%)
  Pallas kernels  10.9 us (31%)
  waiting for transfers between devices  7.31 us (21%)
  other arithmetic  2.99 us (8%)
  local copies, waits for them, and re-layouts  0.43 us (1%)
    ppermute x10, starting transfers between devices, sent(): return lax.ppermute(x, ('tile', 'pgroup'), pairs)  13.2 us
    pallas_call x2, Pallas kernels, profiles(): pl.pallas_call(functools.partial(profile_kernel, pulse_dev, rows, range_r...  8.85 us
    ppermute x10, waiting for transfers between devices, sent(): return lax.ppermute(x, ('tile', 'pgroup'), pairs)  7.31 us
    reshape x1, other arithmetic, per_device(): spread = spread.reshape(pulse_dev, 2 * range_rows, LANES)  2.08 us
    pallas_call x1, Pallas kernels, per_device(): pl.pallas_call(functools.partial(project_kernel, count, normaliser), out_...  1.23 us
    concatenate x1, other arithmetic, where(): pair = jnp.concatenate([offsets, phase_index], axis=0)  0.86 us
    pallas_call x1, Pallas kernels, per_device(): pl.pallas_call(functools.partial(table_kernel, count, pulse_dev), out_sha...  0.78 us
  transfers between devices with their start and end apart: 10, of which 5 were waited for; matrix products, arithmetic and copies ran while one was open for 7% of the time, Pallas kernels for 28%

profile of v1, /device:TPU:0, one launch (start us, length us, event | category | flops | bytes accessed | tf_op | source)
XLA Modules:
  0.0 34.9 jit_solution(443636188797947527)
XLA Ops:
  0.0 0.9 %fusion.2 = (s32[2,64]{1,0:T(2,128)S(1)}, s32[1,2,64]{2,1,0:T(2,128)S(1)}, s32[2,64]{1,0:T(2,128)S(1)}, s32[2,64]{1,0:T(2,128)S(1)}) fusion(s32[]{:T(128)S(6)} %select_n.98, s32[1,1024]{1,0:T(1,128)} %param.6, s32[1,1024]{1,0:T(1,128)} %param.7, s32[]{:T(128)S(6)} %select_n.96, s32[]{:T(128)S(6)} %select_n.100, s32[]{:T(128)S(6)} %select_n.102), kind=kLoop, calls=%fused_computation.20 | loop fusion | flops 512 | bytes 10256 | tf_op jit(solution)/shard_map/concatenate | solution.py:129
  0.9 4.5 %collective-permute-start.3 = (s32[2,64]{1,0:T(2,128)S(1)}, s32[2,64]{1,0:T(2,128)S(1)}, u32[]{:S(2)}, u32[]{:S(2)}) collective-permute-start(s32[2,64]{1,0:T(2,128)S(1)} %get-tuple-element.32), channel_id=1, source_target_pairs={{0,26},{1,27},{2,28},{3,29},{4,30},{5,31},{6,0},{7,1},{8,2},{9,3},... | collective-permute-start | bytes 1544 | tf_op jit(solution)/shard_map/ppermute | solution.py:125
  5.4 1.6 %collective-permute-start.2 = (s32[2,64]{1,0:T(2,128)S(1)}, s32[2,64]{1,0:T(2,128)S(1)}, u32[]{:S(2)}, u32[]{:S(2)}) collective-permute-start(s32[2,64]{1,0:T(2,128)S(1)} %get-tuple-element.31), channel_id=1, source_target_pairs={{0,28},{1,29},{2,30},{3,31},{4,0},{5,1},{6,2},{7,3},{8,4},{9,5},{1... | collective-permute-start | bytes 1544 | tf_op jit(solution)/shard_map/ppermute | solution.py:125
  7.0 1.3 %collective-permute-start.1 = (s32[2,64]{1,0:T(2,128)S(1)}, s32[2,64]{1,0:T(2,128)S(1)}, u32[]{:S(2)}, u32[]{:S(2)}) collective-permute-start(s32[2,64]{1,0:T(2,128)S(1)} %get-tuple-element.29), channel_id=1, source_target_pairs={{0,30},{1,31},{2,0},{3,1},{4,2},{5,3},{6,4},{7,5},{8,6},{9,7},{10,... | collective-permute-start | bytes 1544 | tf_op jit(solution)/shard_map/ppermute | solution.py:125
  8.3 2.1 %bitcast_convert_fusion = f32[64,2,32,128]{3,1,2,0:T(2,128)S(1)} fusion(bf16[64,2,4096]{2,1,0:T(2,128)(2,1)} %param.5), kind=kLoop, calls=%fused_computation | loop fusion | flops 524288 | bytes 3145728 | tf_op jit(solution)/shard_map/reshape | solution.py:134
  10.4 0.0 copy-done.1
  10.4 0.1 copy.26.kern_ref
  10.4 2.5 %profiles.2 = (bf16[256,128]{1,0:T(8,128)(2,1)S(1)}, bf16[256,128]{1,0:T(8,128)(2,1)S(1)}) custom-call(s32[1,2,64]{2,1,0:T(2,128)S(1)} %get-tuple-element.30.where_ref, s32[1]{0:T(128)} %bitcast.1.group_ref, f32[16,8]{1,0:T(8,128)S(1)} %copy.26.kern_ref, f32[64,64,128]{2,1,0:T(8,128)S(1)} %bitcast.37), custom_call_target="tpu_custom_call" | custom-call | tf_op jit(solution)/shard_map/profiles/pallas_call | solution.py:140
  12.9 1.6 %collective-permute-start = (bf16[256,128]{1,0:T(8,128)(2,1)S(1)}, bf16[256,128]{1,0:T(8,128)(2,1)S(1)}, u32[]{:S(2)}, u32[]{:S(2)}) collective-permute-start(bf16[256,128]{1,0:T(8,128)(2,1)S(1)} %get-tuple-element.14), channel_id=1, source_target_pairs={{0,1},{1,0},{2,3},{3,2},{4,5},{5,4},{6,7},{7,6},{8,9},{9,8},{10,11... | collective-permute-start | bytes 196616 | tf_op jit(solution)/shard_map/ppermute | solution.py:125
  14.5 0.0 collective-permute-done.3
  14.5 0.0 collective-permute-done.2
  14.5 0.0 collective-permute-done.1
  14.5 6.4 %profiles.3 = (bf16[256,128]{1,0:T(8,128)(2,1)S(1)}, bf16[256,128]{1,0:T(8,128)(2,1)S(1)}, bf16[256,128]{1,0:T(8,128)(2,1)S(1)}, bf16[256,128]{1,0:T(8,128)(2,1)...) custom-call(s32[3,2,64]{2,1,0:T(2,128)S(1)} %pad_add_fusion.where_ref, s32[1]{0:T(128)} %bitcast.1.group_ref, ...), custom_call_target="tpu_custom_call" | custom-call | tf_op jit(solution)/shard_map/profiles/pallas_call | solution.py:140
  20.9 0.1 collective-permute-start.4
  21.0 0.0 copy-done
  21.1 0.1 reshape_squeeze.3
  21.2 0.8 %collective-permute-start.5 = (bf16[256,128]{1,0:T(8,128)(2,1)S(1)}, bf16[256,128]{1,0:T(8,128)(2,1)S(1)}, u32[]{:S(2)}, u32[]{:S(2)}) collective-permute-start(bf16[256,128]{1,0:T(8,128)(2,1)S(1)} %get-tuple-element.16), channel_id=1, source_target_pairs={{0,3},{1,2},{2,5},{3,4},{4,7},{5,6},{6,9},{7,8},{8,11},{9,10},{10,... | collective-permute-start | bytes 196616 | tf_op jit(solution)/shard_map/ppermute | solution.py:125
  22.0 2.4 %collective-permute-start.6 = (bf16[256,128]{1,0:T(8,128)(2,1)S(1)}, bf16[256,128]{1,0:T(8,128)(2,1)S(1)}, u32[]{:S(2)}, u32[]{:S(2)}) collective-permute-start(bf16[256,128]{1,0:T(8,128)(2,1)S(1)} %get-tuple-element.17), channel_id=1, source_target_pairs={{0,4},{1,5},{2,6},{3,7},{4,8},{5,9},{6,10},{7,11},{8,12},{9,13},{1... | collective-permute-start | bytes 196616 | tf_op jit(solution)/shard_map/ppermute | solution.py:125
  24.4 0.9 %collective-permute-start.7 = (bf16[256,128]{1,0:T(8,128)(2,1)S(1)}, bf16[256,128]{1,0:T(8,128)(2,1)S(1)}, u32[]{:S(2)}, u32[]{:S(2)}) collective-permute-start(bf16[256,128]{1,0:T(8,128)(2,1)S(1)} %get-tuple-element.18), channel_id=1, source_target_pairs={{0,5},{1,4},{2,7},{3,6},{4,9},{5,8},{6,11},{7,10},{8,13},{9,12},{1... | collective-permute-start | bytes 196616 | tf_op jit(solution)/shard_map/ppermute | solution.py:125
  25.3 0.0 collective-permute-done.refs_1_
  25.3 0.0 collective-permute-start.8
  25.3 2.0 %collective-permute-done.4.refs_2_ = bf16[256,128]{1,0:T(8,128)(2,1)S(1)} collective-permute-done((bf16[256,128]{1,0:T(8,128)(2,1)S(1)}, bf16[256,128]{1,0:T(8,128)(2,1)S(1)}, u32[]{:S(2)}, u32[]{:S(2)}) %collective-permute-start.4) | collective-permute-done | bytes 65568 | tf_op jit(solution)/shard_map/ppermute | solution.py:125
  27.3 0.0 collective-permute-start.9
  27.4 0.1 concatenate.10
  27.5 0.1 copy.36
  27.6 0.8 %steering_table.1.refs_8_ = bf16[1024,512]{1,0:T(8,128)(2,1)S(1)} custom-call(f32[512,2]{1,0:T(8,128)S(1)} %bitcast.39), custom_call_target="tpu_custom_call" | custom-call | tf_op jit(solution)/shard_map/steering_table/pallas_call | solution.py:162
  28.4 0.5 %collective-permute-done.5.refs_3_ = bf16[256,128]{1,0:T(8,128)(2,1)S(1)} collective-permute-done((bf16[256,128]{1,0:T(8,128)(2,1)S(1)}, bf16[256,128]{1,0:T(8,128)(2,1)S(1)}, u32[]{:S(2)}, u32[]{:S(2)}) %collective-permute-start.5) | collective-permute-done | bytes 65568 | tf_op jit(solution)/shard_map/ppermute | solution.py:125
  28.9 1.0 %collective-permute-done.6.refs_4_ = bf16[256,128]{1,0:T(8,128)(2,1)S(1)} collective-permute-done((bf16[256,128]{1,0:T(8,128)(2,1)S(1)}, bf16[256,128]{1,0:T(8,128)(2,1)S(1)}, u32[]{:S(2)}, u32[]{:S(2)}) %collective-permute-start.6) | collective-permute-done | bytes 65568 | tf_op jit(solution)/shard_map/ppermute | solution.py:125
  29.9 3.2 %collective-permute-done.7.refs_5_ = bf16[256,128]{1,0:T(8,128)(2,1)S(1)} collective-permute-done((bf16[256,128]{1,0:T(8,128)(2,1)S(1)}, bf16[256,128]{1,0:T(8,128)(2,1)S(1)}, u32[]{:S(2)}, u32[]{:S(2)}) %collective-permute-start.7) | collective-permute-done | bytes 65568 | tf_op jit(solution)/shard_map/ppermute | solution.py:125
  33.0 0.0 collective-permute-done.8.refs_6_
  33.0 0.7 %collective-permute-done.9.refs_7_ = bf16[256,128]{1,0:T(8,128)(2,1)S(1)} collective-permute-done((bf16[256,128]{1,0:T(8,128)(2,1)S(1)}, bf16[256,128]{1,0:T(8,128)(2,1)S(1)}, u32[]{:S(2)}, u32[]{:S(2)}) %collective-permute-start.9) | collective-permute-done | bytes 65568 | tf_op jit(solution)/shard_map/ppermute | solution.py:125
  33.7 1.2 %project.1 = f32[2,256,256]{2,1,0:T(8,128)} custom-call(bf16[256,128]{1,0:T(8,128)(2,1)S(1)} %get-tuple-element.13.refs_0_, bf16[256,128]{1,0:T(8,128)(2,1)S(1)} %collective-permute-done.refs_1_, bf16[256,128]{1,0:T(8,128)(2,1)S(1)} %collective-permute-done.4.refs_2_, bf16[256,128]{1,0:T(8,128)(2,1)S(1)} %collective-permute-done.5.refs_3_, ...), custom_call_target="tpu_custom_call" | custom-call | tf_op jit(solution)/shard_map/project/pallas_call | solution.py:176
  (5 shorter events, 0.1 us)
Async XLA Ops:
  0.0 10.4 %copy-start.1 = (f32[16,8]{0,1:T(8,128)S(1)}, f32[16,8]{0,1:T(8,128)}, u32[]{:S(2)}) copy-start(f32[16,8]{0,1:T(8,128)} %param.9) | copy-start | bytes 1540
  0.9 13.6 %collective-permute-start.3 = (s32[2,64]{1,0:T(2,128)S(1)}, s32[2,64]{1,0:T(2,128)S(1)}, u32[]{:S(2)}, u32[]{:S(2)}) collective-permute-start(s32[2,64]{1,0:T(2,128)S(1)} %get-tuple-element.32), channel_id=1, source_target_pairs={{0,26},{1,27},{2,28},{3,29},{4,30},{5,31},{6,0},{7,1},{8,2},{9,3},... | collective-permute-start | bytes 1544 | tf_op jit(solution)/shard_map/ppermute | solution.py:125
  5.4 9.1 %collective-permute-start.2 = (s32[2,64]{1,0:T(2,128)S(1)}, s32[2,64]{1,0:T(2,128)S(1)}, u32[]{:S(2)}, u32[]{:S(2)}) collective-permute-start(s32[2,64]{1,0:T(2,128)S(1)} %get-tuple-element.31), channel_id=1, source_target_pairs={{0,28},{1,29},{2,30},{3,31},{4,0},{5,1},{6,2},{7,3},{8,4},{9,5},{1... | collective-permute-start | bytes 1544 | tf_op jit(solution)/shard_map/ppermute | solution.py:125
  7.0 7.5 %collective-permute-start.1 = (s32[2,64]{1,0:T(2,128)S(1)}, s32[2,64]{1,0:T(2,128)S(1)}, u32[]{:S(2)}, u32[]{:S(2)}) collective-permute-start(s32[2,64]{1,0:T(2,128)S(1)} %get-tuple-element.29), channel_id=1, source_target_pairs={{0,30},{1,31},{2,0},{3,1},{4,2},{5,3},{6,4},{7,5},{8,6},{9,7},{10,... | collective-permute-start | bytes 1544 | tf_op jit(solution)/shard_map/ppermute | solution.py:125
  10.4 10.6 %copy-start = (f32[2,1,2048]{2,1,0:T(1,128)S(1)}, f32[2,1,2048]{2,1,0:T(1,128)}, u32[]{:S(2)}) copy-start(f32[2,1,2048]{2,1,0:T(1,128)} %param.8) | copy-start | bytes 49156
  12.9 12.4 %collective-permute-start = (bf16[256,128]{1,0:T(8,128)(2,1)S(1)}, bf16[256,128]{1,0:T(8,128)(2,1)S(1)}, u32[]{:S(2)}, u32[]{:S(2)}) collective-permute-start(bf16[256,128]{1,0:T(8,128)(2,1)S(1)} %get-tuple-element.14), channel_id=1, source_target_pairs={{0,1},{1,0},{2,3},{3,2},{4,5},{5,4},{6,7},{7,6},{8,9},{9,8},{10,11... | collective-permute-start | bytes 196616 | tf_op jit(solution)/shard_map/ppermute | solution.py:125
  20.9 6.4 %collective-permute-start.4 = (bf16[256,128]{1,0:T(8,128)(2,1)S(1)}, bf16[256,128]{1,0:T(8,128)(2,1)S(1)}, u32[]{:S(2)}, u32[]{:S(2)}) collective-permute-start(bf16[256,128]{1,0:T(8,128)(2,1)S(1)} %get-tuple-element.15), channel_id=1, source_target_pairs={{0,2},{1,3},{2,4},{3,5},{4,6},{5,7},{6,8},{7,9},{8,10},{9,11},{10,... | collective-permute-start | bytes 196616 | tf_op jit(solution)/shard_map/ppermute | solution.py:125
  21.2 7.8 %collective-permute-start.5 = (bf16[256,128]{1,0:T(8,128)(2,1)S(1)}, bf16[256,128]{1,0:T(8,128)(2,1)S(1)}, u32[]{:S(2)}, u32[]{:S(2)}) collective-permute-start(bf16[256,128]{1,0:T(8,128)(2,1)S(1)} %get-tuple-element.16), channel_id=1, source_target_pairs={{0,3},{1,2},{2,5},{3,4},{4,7},{5,6},{6,9},{7,8},{8,11},{9,10},{10,... | collective-permute-start | bytes 196616 | tf_op jit(solution)/shard_map/ppermute | solution.py:125
  22.0 7.9 %collective-permute-start.6 = (bf16[256,128]{1,0:T(8,128)(2,1)S(1)}, bf16[256,128]{1,0:T(8,128)(2,1)S(1)}, u32[]{:S(2)}, u32[]{:S(2)}) collective-permute-start(bf16[256,128]{1,0:T(8,128)(2,1)S(1)} %get-tuple-element.17), channel_id=1, source_target_pairs={{0,4},{1,5},{2,6},{3,7},{4,8},{5,9},{6,10},{7,11},{8,12},{9,13},{1... | collective-permute-start | bytes 196616 | tf_op jit(solution)/shard_map/ppermute | solution.py:125
  24.4 8.6 %collective-permute-start.7 = (bf16[256,128]{1,0:T(8,128)(2,1)S(1)}, bf16[256,128]{1,0:T(8,128)(2,1)S(1)}, u32[]{:S(2)}, u32[]{:S(2)}) collective-permute-start(bf16[256,128]{1,0:T(8,128)(2,1)S(1)} %get-tuple-element.18), channel_id=1, source_target_pairs={{0,5},{1,4},{2,7},{3,6},{4,9},{5,8},{6,11},{7,10},{8,13},{9,12},{1... | collective-permute-start | bytes 196616 | tf_op jit(solution)/shard_map/ppermute | solution.py:125
  25.3 7.7 %collective-permute-start.8 = (bf16[256,128]{1,0:T(8,128)(2,1)S(1)}, bf16[256,128]{1,0:T(8,128)(2,1)S(1)}, u32[]{:S(2)}, u32[]{:S(2)}) collective-permute-start(bf16[256,128]{1,0:T(8,128)(2,1)S(1)} %get-tuple-element.19), channel_id=1, source_target_pairs={{0,6},{1,7},{2,8},{3,9},{4,10},{5,11},{6,12},{7,13},{8,14},{9,15},... | collective-permute-start | bytes 196616 | tf_op jit(solution)/shard_map/ppermute | solution.py:125
  27.3 6.4 %collective-permute-start.9 = (bf16[256,128]{1,0:T(8,128)(2,1)S(1)}, bf16[256,128]{1,0:T(8,128)(2,1)S(1)}, u32[]{:S(2)}, u32[]{:S(2)}) collective-permute-start(bf16[256,128]{1,0:T(8,128)(2,1)S(1)} %get-tuple-element.20), channel_id=1, source_target_pairs={{0,7},{1,6},{2,9},{3,8},{4,11},{5,10},{6,13},{7,12},{8,15},{9,14},... | collective-permute-start | bytes 196616 | tf_op jit(solution)/shard_map/ppermute | solution.py:125

commit v2 on v1

--- a/solution.py
+++ b/solution.py
@@ -61,42 +61,52 @@
         table_ref[at + pulse_dev : at + 2 * pulse_dev, columns:] = c16
 
 
-def profile_kernel(pulse_dev, rows, range_rows, taps, groups, count, where_ref, group_ref, kern_ref, echo_ref, *rest):
-    outs, scratch = rest[:-1], rest[-1]
+def profile_kernel(pulse_dev, rows, taps, phases, groups, count, at_ref, group_ref, phase_ref, kern_ref, echo_ref, *rest):
+    outs, (wide, tail, turned) = rest[:-3], rest[-3:]
     tall = 2 * rows // LANES
     lane = lax.broadcasted_iota(jnp.int32, (tall, LANES), 1)
-    top = 2 * (range_rows - rows // LANES)
     me = group_ref[0]
+    total = count * pulse_dev
 
     for i in range(count):
 
-        def one(p, carry, i=i):
-            first = where_ref[i, 0, p]
-            phase = where_ref[i, 1, p]
-            a = lax.shift_right_logical(first, 7) * 2
-            b = jnp.bitwise_and(first, LANES - 1)
-            x0 = echo_ref[p, pl.ds(a, tall), :]
-            x1 = echo_ref[p, pl.ds(a + 2, tall), :]
-            x2 = echo_ref[p, pl.ds(jnp.minimum(a + 4, top), tall), :]
+        def align(p, carry, i=i):
+            k = i * pulse_dev + p
+            first, last, b = at_ref[k], at_ref[total + k], at_ref[2 * total + k]
+            x0 = echo_ref[pl.ds(first, tall), :]
+            x1 = echo_ref[pl.ds(first + 2, tall), :]
+            x2 = echo_ref[pl.ds(last, 8), :]
             keep = lane >= b
             turn = LANES - b
-            w0 = pltpu.roll(jnp.where(keep, x0, x1), turn, 1)
-            w1 = pltpu.roll(jnp.where(keep, x1, x2), turn, 1)
-            total = kern_ref[phase, 0] * w0
-            for j in range(1, taps):
-                shifted = pltpu.roll(jnp.where(lane >= j, w0, w1), LANES - j, 1)
-                total = total + kern_ref[phase, j] * shifted
-            scratch[pl.ds(p * tall, tall), :] = total
+            wide[pl.ds(pl.multiple_of(p * tall, 8), tall), :] = pltpu.roll(jnp.where(keep, x0, x1), turn, 1)
+            end = jnp.where(keep[tall - 8 :], x1[tall - 8 :], x2)
+            tail[pl.ds(pl.multiple_of(p * 8, 8), 8), :] = pltpu.roll(end, turn, 1)
             return carry
 
-        lax.fori_loop(0, pulse_dev, one, 0, unroll=8)
+        lax.fori_loop(0, pulse_dev, align, 0, unroll=32)
+        for r in range(rows // LANES):
+            both = [wide[pl.ds(2 * r + q, pulse_dev, stride=tall), :] for q in range(2)]
+            turned[r * LANES : (r + 1) * LANES, :] = jnp.concatenate(both, axis=0).T
+        both = [tail[pl.ds(6 + q, pulse_dev, stride=8), :] for q in range(2)]
+        turned[rows : rows + 8, :] = jnp.concatenate(both, axis=0).T[:8]
+
+        phase = jnp.broadcast_to(phase_ref[i], (taps, 2 * pulse_dev))
+        kern = kern_ref[0]
+        for h in range(1, phases):
+            kern = jnp.where(phase == h, kern_ref[h], kern)
+        kern = [jnp.broadcast_to(kern[j : j + 1], (16, 2 * pulse_dev)) for j in range(taps)]
         for f in range(groups):
-            half = lax.rem(me + f, groups)
-            per = ROW_DEV // LANES
-            for r in range(per):
-                parts = [scratch[pl.ds(half * (2 * per) + 2 * r + q, pulse_dev, stride=tall), :] for q in range(2)]
-                both = jnp.concatenate(parts, axis=0)
-                outs[i * groups + f][r * LANES : (r + 1) * LANES, :] = both.T.astype(jnp.bfloat16)
+            base = lax.rem(me + f, groups) * ROW_DEV
+
+            def fir(m, carry, out=outs[i * groups + f], base=base):
+                at = pl.multiple_of(m * 16, 16)
+                summed = kern[0] * turned[pl.ds(base + at, 16), :]
+                for j in range(1, taps):
+                    summed = summed + kern[j] * turned[pl.ds(base + at + j, 16), :]
+                out[pl.ds(at, 16), :] = summed.astype(jnp.bfloat16)
+                return carry
+
+            lax.fori_loop(0, ROW_DEV // 16, fir, 0, unroll=4)
 
 
 def project_kernel(count, normaliser, *refs):
@@ -131,21 +141,35 @@
 
     asked = [sent(where(d), -d, 0) for d in range(1, STEPS)]
     spread = echoes.reshape(pulse_dev, 2, range_rows, LANES).transpose(0, 2, 1, 3).astype(jnp.float32)
-    spread = spread.reshape(pulse_dev, 2 * range_rows, LANES)
+    spread = spread.reshape(pulse_dev * 2 * range_rows, LANES)
     me = group.reshape(1)
+
+    phases = kernels.shape[0]
+    kern = jnp.broadcast_to(kernels[:, :, None], (phases, taps, 2 * pulse_dev))
 
     def profiles(wheres):
         count = wheres.shape[0]
+        tall = 2 * rows // LANES
+        firsts = wheres[:, 0].reshape(-1)
+        sample_row = 2 * (firsts // LANES)
+        pulse_row = jnp.arange(count * pulse_dev, dtype=jnp.int32) % pulse_dev * (2 * range_rows)
+        ends = jnp.minimum(sample_row + 4 + tall - 8, 2 * range_rows - 8)
+        at = jnp.concatenate([pulse_row + sample_row, pulse_row + ends, firsts % LANES])
+        phase = jnp.concatenate([wheres[:, 1:], wheres[:, 1:]], axis=2)
         shape = jax.ShapeDtypeStruct((ROW_DEV, 2 * pulse_dev), jnp.bfloat16)
         return pl.pallas_call(
-            functools.partial(profile_kernel, pulse_dev, rows, range_rows, taps, group_count, count),
+            functools.partial(profile_kernel, pulse_dev, rows, taps, phases, group_count, count),
             out_shape=[shape] * (count * group_count),
-            in_specs=[whole(pltpu.SMEM), whole(pltpu.SMEM), whole(pltpu.SMEM), whole()],
+            in_specs=[whole(pltpu.SMEM), whole(pltpu.SMEM), whole(), whole(), whole()],
             out_specs=[whole()] * (count * group_count),
-            scratch_shapes=[pltpu.VMEM((pulse_dev * 2 * rows // LANES, LANES), jnp.float32)],
+            scratch_shapes=[
+                pltpu.VMEM((pulse_dev * tall, LANES), jnp.float32),
+                pltpu.VMEM((pulse_dev * 8, LANES), jnp.float32),
+                pltpu.VMEM((rows + 8, 2 * pulse_dev), jnp.float32),
+            ],
             compiler_params=pltpu.CompilerParams(vmem_limit_bytes=24 * 1024 * 1024),
             name="profiles",
-        )(wheres, me, kernels, spread)
+        )(at, me, phase, kern, spread)
 
     own = profiles(where(0)[None])
     arrived = [[own[0]] + [sent(own[f], 0, f) for f in range(1, group_count)]]

time: 35.3 us -> 30.6 us (0.87)
  Pallas kernels: 10.9 us -> 5.7 us
    pallas_call x2, Pallas kernels: 8.85 us -> 3.69 us  [profiles(): pl.pallas_call(functools.partial(profile_kernel, pulse_dev, rows, taps, p...]
  transfers between devices with their start and end apart: 10 -> 10, of which waited for: 5 -> 5; matrix products, arithmetic and copies ran while one was open for 7% -> 10% of each run, Pallas kernels for 28% -> 15%
where the time goes in v2:
time: 30.6 us; the launch traced here: 30.3 us
  starting transfers between devices  13.2 us (43%)
  waiting for transfers between devices  7.31 us (24%)
  Pallas kernels  5.7 us (19%)
  other arithmetic  3.33 us (11%)
  local copies, waits for them, and re-layouts  0.62 us (2%)
    ppermute x10, starting transfers between devices, sent(): return lax.ppermute(x, ('tile', 'pgroup'), pairs)  13.2 us
    ppermute x10, waiting for transfers between devices, sent(): return lax.ppermute(x, ('tile', 'pgroup'), pairs)  7.31 us
    pallas_call x2, Pallas kernels, profiles(): pl.pallas_call(functools.partial(profile_kernel, pulse_dev, rows, taps, p...  3.69 us
    reshape x1, other arithmetic, per_device(): spread = spread.reshape(pulse_dev * 2 * range_rows, LANES)  2.08 us
    pallas_call x1, Pallas kernels, per_device(): pl.pallas_call(functools.partial(project_kernel, count, normaliser), out_...  1.23 us
    concatenate x1, other arithmetic, where(): pair = jnp.concatenate([offsets, phase_index], axis=0)  0.86 us
    pallas_call x1, Pallas kernels, per_device(): pl.pallas_call(functools.partial(table_kernel, count, pulse_dev), out_sha...  0.78 us
  transfers between devices with their start and end apart: 10, of which 5 were waited for; matrix products, arithmetic and copies ran while one was open for 10% of the time, Pallas kernels for 15%

profile of v2, /device:TPU:0, one launch (start us, length us, event | category | flops | bytes accessed | tf_op | source)
XLA Modules:
  0.0 30.3 jit_solution(1186971607986216385)
XLA Ops:
  0.0 0.9 %fusion.2 = (s32[2,64]{1,0:T(2,128)S(1)}, s32[1,2,64]{2,1,0:T(2,128)S(1)}, s32[2,64]{1,0:T(2,128)S(1)}, s32[2,64]{1,0:T(2,128)S(1)}) fusion(s32[]{:T(128)S(6)} %select_n.136, s32[1,1024]{1,0:T(1,128)} %param.6, s32[1,1024]{1,0:T(1,128)} %param.7, s32[]{:T(128)S(6)} %select_n.131, s32[]{:T(128)S(6)} %select_n.138, s32[]{:T(128)S(6)} %select_n.140), kind=kLoop, calls=%fused_computation.35 | loop fusion | flops 512 | bytes 10256 | tf_op jit(solution)/shard_map/concatenate | solution.py:139
  0.9 4.5 %collective-permute-start.3 = (s32[2,64]{1,0:T(2,128)S(1)}, s32[2,64]{1,0:T(2,128)S(1)}, u32[]{:S(2)}, u32[]{:S(2)}) collective-permute-start(s32[2,64]{1,0:T(2,128)S(1)} %get-tuple-element.37), channel_id=1, source_target_pairs={{0,26},{1,27},{2,28},{3,29},{4,30},{5,31},{6,0},{7,1},{8,2},{9,3},... | collective-permute-start | bytes 1544 | tf_op jit(solution)/shard_map/ppermute | solution.py:135
  5.4 1.6 %collective-permute-start.2 = (s32[2,64]{1,0:T(2,128)S(1)}, s32[2,64]{1,0:T(2,128)S(1)}, u32[]{:S(2)}, u32[]{:S(2)}) collective-permute-start(s32[2,64]{1,0:T(2,128)S(1)} %get-tuple-element.36), channel_id=1, source_target_pairs={{0,28},{1,29},{2,30},{3,31},{4,0},{5,1},{6,2},{7,3},{8,4},{9,5},{1... | collective-permute-start | bytes 1544 | tf_op jit(solution)/shard_map/ppermute | solution.py:135
  7.0 1.3 %collective-permute-start.1 = (s32[2,64]{1,0:T(2,128)S(1)}, s32[2,64]{1,0:T(2,128)S(1)}, u32[]{:S(2)}, u32[]{:S(2)}) collective-permute-start(s32[2,64]{1,0:T(2,128)S(1)} %get-tuple-element.34), channel_id=1, source_target_pairs={{0,30},{1,31},{2,0},{3,1},{4,2},{5,3},{6,4},{7,5},{8,6},{9,7},{10,... | collective-permute-start | bytes 1544 | tf_op jit(solution)/shard_map/ppermute | solution.py:135
  8.3 0.1 pad_add_fusion.4.phase_ref
  8.4 2.1 %bitcast_convert_fusion = f32[64,2,32,128]{3,1,2,0:T(2,128)S(1)} fusion(bf16[64,2,4096]{2,1,0:T(2,128)(2,1)} %param.5), kind=kLoop, calls=%fused_computation | loop fusion | flops 524288 | bytes 3145728 | tf_op jit(solution)/shard_map/reshape | solution.py:144
  10.5 0.1 pad_add_fusion.3.at_ref
  10.5 0.1 copy.24
  10.6 0.1 broadcast_in_dim.10.kern_ref
  10.7 1.2 %profiles.2 = (bf16[256,128]{1,0:T(8,128)(2,1)S(1)}, bf16[256,128]{1,0:T(8,128)(2,1)S(1)}) custom-call(s32[192]{0:T(256)S(1)} %pad_add_fusion.3.at_ref, s32[1]{0:T(128)} %bitcast.2.group_ref, s32[1,1,128]{2,1,0:T(1,128)S(1)} %pad_add_fusion.4.phase_ref, f32[16,8,128]{2,1,0:T(8,128)S(1)} %broadcast_in_dim.10.kern_ref, f32[4096,128]{1,0:T(8,128)S(1)} %bitcast.52), custom_call_target="tpu_custom_call" | custom-call | tf_op jit(solution)/shard_map/profiles/pallas_call | solution.py:160
  11.9 1.6 %collective-permute-start = (bf16[256,128]{1,0:T(8,128)(2,1)S(1)}, bf16[256,128]{1,0:T(8,128)(2,1)S(1)}, u32[]{:S(2)}, u32[]{:S(2)}) collective-permute-start(bf16[256,128]{1,0:T(8,128)(2,1)S(1)} %get-tuple-element.14), channel_id=1, source_target_pairs={{0,1},{1,0},{2,3},{3,2},{4,5},{5,4},{6,7},{7,6},{8,9},{9,8},{10,11... | collective-permute-start | bytes 196616 | tf_op jit(solution)/shard_map/ppermute | solution.py:135
  13.4 0.0 collective-permute-done.3
  13.5 0.0 collective-permute-done.2
  13.5 0.0 collective-permute-done.1
  13.5 0.1 reshape_squeeze.10
  13.6 0.1 pad_add_fusion.at_ref
  13.7 0.1 pad_add_fusion.2.phase_ref
  13.8 2.5 %profiles.3 = (bf16[256,128]{1,0:T(8,128)(2,1)S(1)}, bf16[256,128]{1,0:T(8,128)(2,1)S(1)}, bf16[256,128]{1,0:T(8,128)(2,1)S(1)}, bf16[256,128]{1,0:T(8,128)(2,1)...) custom-call(s32[576]{0:T(1024)S(1)} %pad_add_fusion.at_ref, s32[1]{0:T(128)} %bitcast.2.group_ref, ...), custom_call_target="tpu_custom_call" | custom-call | tf_op jit(solution)/shard_map/profiles/pallas_call | solution.py:160
  16.3 0.1 collective-permute-start.4
  16.4 0.1 reshape_squeeze.11
  16.5 0.8 %collective-permute-start.5 = (bf16[256,128]{1,0:T(8,128)(2,1)S(1)}, bf16[256,128]{1,0:T(8,128)(2,1)S(1)}, u32[]{:S(2)}, u32[]{:S(2)}) collective-permute-start(bf16[256,128]{1,0:T(8,128)(2,1)S(1)} %get-tuple-element.16), channel_id=1, source_target_pairs={{0,3},{1,2},{2,5},{3,4},{4,7},{5,6},{6,9},{7,8},{8,11},{9,10},{10,... | collective-permute-start | bytes 196616 | tf_op jit(solution)/shard_map/ppermute | solution.py:135
  17.4 2.4 %collective-permute-start.6 = (bf16[256,128]{1,0:T(8,128)(2,1)S(1)}, bf16[256,128]{1,0:T(8,128)(2,1)S(1)}, u32[]{:S(2)}, u32[]{:S(2)}) collective-permute-start(bf16[256,128]{1,0:T(8,128)(2,1)S(1)} %get-tuple-element.17), channel_id=1, source_target_pairs={{0,4},{1,5},{2,6},{3,7},{4,8},{5,9},{6,10},{7,11},{8,12},{9,13},{1... | collective-permute-start | bytes 196616 | tf_op jit(solution)/shard_map/ppermute | solution.py:135
  19.8 0.9 %collective-permute-start.7 = (bf16[256,128]{1,0:T(8,128)(2,1)S(1)}, bf16[256,128]{1,0:T(8,128)(2,1)S(1)}, u32[]{:S(2)}, u32[]{:S(2)}) collective-permute-start(bf16[256,128]{1,0:T(8,128)(2,1)S(1)} %get-tuple-element.18), channel_id=1, source_target_pairs={{0,5},{1,4},{2,7},{3,6},{4,9},{5,8},{6,11},{7,10},{8,13},{9,12},{1... | collective-permute-start | bytes 196616 | tf_op jit(solution)/shard_map/ppermute | solution.py:135
  20.7 2.0 %collective-permute-done.4.refs_2_ = bf16[256,128]{1,0:T(8,128)(2,1)S(1)} collective-permute-done((bf16[256,128]{1,0:T(8,128)(2,1)S(1)}, bf16[256,128]{1,0:T(8,128)(2,1)S(1)}, u32[]{:S(2)}, u32[]{:S(2)}) %collective-permute-start.4) | collective-permute-done | bytes 65568 | tf_op jit(solution)/shard_map/ppermute | solution.py:135
  22.7 0.1 concatenate.26
  22.8 0.1 copy.34
  23.0 0.8 %steering_table.1.refs_8_ = bf16[1024,512]{1,0:T(8,128)(2,1)S(1)} custom-call(f32[512,2]{1,0:T(8,128)S(1)} %bitcast.54), custom_call_target="tpu_custom_call" | custom-call | tf_op jit(solution)/shard_map/steering_table/pallas_call | solution.py:186
  23.8 0.5 %collective-permute-done.5.refs_3_ = bf16[256,128]{1,0:T(8,128)(2,1)S(1)} collective-permute-done((bf16[256,128]{1,0:T(8,128)(2,1)S(1)}, bf16[256,128]{1,0:T(8,128)(2,1)S(1)}, u32[]{:S(2)}, u32[]{:S(2)}) %collective-permute-start.5) | collective-permute-done | bytes 65568 | tf_op jit(solution)/shard_map/ppermute | solution.py:135
  24.3 1.0 %collective-permute-done.6.refs_4_ = bf16[256,128]{1,0:T(8,128)(2,1)S(1)} collective-permute-done((bf16[256,128]{1,0:T(8,128)(2,1)S(1)}, bf16[256,128]{1,0:T(8,128)(2,1)S(1)}, u32[]{:S(2)}, u32[]{:S(2)}) %collective-permute-start.6) | collective-permute-done | bytes 65568 | tf_op jit(solution)/shard_map/ppermute | solution.py:135
  25.3 3.2 %collective-permute-done.7.refs_5_ = bf16[256,128]{1,0:T(8,128)(2,1)S(1)} collective-permute-done((bf16[256,128]{1,0:T(8,128)(2,1)S(1)}, bf16[256,128]{1,0:T(8,128)(2,1)S(1)}, u32[]{:S(2)}, u32[]{:S(2)}) %collective-permute-start.7) | collective-permute-done | bytes 65568 | tf_op jit(solution)/shard_map/ppermute | solution.py:135
  28.4 0.7 %collective-permute-done.9.refs_7_ = bf16[256,128]{1,0:T(8,128)(2,1)S(1)} collective-permute-done((bf16[256,128]{1,0:T(8,128)(2,1)S(1)}, bf16[256,128]{1,0:T(8,128)(2,1)S(1)}, u32[]{:S(2)}, u32[]{:S(2)}) %collective-permute-start.9) | collective-permute-done | bytes 65568 | tf_op jit(solution)/shard_map/ppermute | solution.py:135
  29.1 1.2 %project.1 = f32[2,256,256]{2,1,0:T(8,128)} custom-call(bf16[256,128]{1,0:T(8,128)(2,1)S(1)} %get-tuple-element.13.refs_0_, bf16[256,128]{1,0:T(8,128)(2,1)S(1)} %collective-permute-done.refs_1_, bf16[256,128]{1,0:T(8,128)(2,1)S(1)} %collective-permute-done.4.refs_2_, bf16[256,128]{1,0:T(8,128)(2,1)S(1)} %collective-permute-done.5.refs_3_, ...), custom_call_target="tpu_custom_call" | custom-call | tf_op jit(solution)/shard_map/project/pallas_call | solution.py:200
  (17 shorter events, 0.2 us)
Async XLA Ops:
  0.0 10.5 %copy-start.1 = (f32[16,8]{0,1:T(8,128)S(1)}, f32[16,8]{0,1:T(8,128)}, u32[]{:S(2)}) copy-start(f32[16,8]{0,1:T(8,128)} %param.9) | copy-start | bytes 1540
  0.9 12.6 %collective-permute-start.3 = (s32[2,64]{1,0:T(2,128)S(1)}, s32[2,64]{1,0:T(2,128)S(1)}, u32[]{:S(2)}, u32[]{:S(2)}) collective-permute-start(s32[2,64]{1,0:T(2,128)S(1)} %get-tuple-element.37), channel_id=1, source_target_pairs={{0,26},{1,27},{2,28},{3,29},{4,30},{5,31},{6,0},{7,1},{8,2},{9,3},... | collective-permute-start | bytes 1544 | tf_op jit(solution)/shard_map/ppermute | solution.py:135
  5.4 8.1 %collective-permute-start.2 = (s32[2,64]{1,0:T(2,128)S(1)}, s32[2,64]{1,0:T(2,128)S(1)}, u32[]{:S(2)}, u32[]{:S(2)}) collective-permute-start(s32[2,64]{1,0:T(2,128)S(1)} %get-tuple-element.36), channel_id=1, source_target_pairs={{0,28},{1,29},{2,30},{3,31},{4,0},{5,1},{6,2},{7,3},{8,4},{9,5},{1... | collective-permute-start | bytes 1544 | tf_op jit(solution)/shard_map/ppermute | solution.py:135
  7.0 6.5 %collective-permute-start.1 = (s32[2,64]{1,0:T(2,128)S(1)}, s32[2,64]{1,0:T(2,128)S(1)}, u32[]{:S(2)}, u32[]{:S(2)}) collective-permute-start(s32[2,64]{1,0:T(2,128)S(1)} %get-tuple-element.34), channel_id=1, source_target_pairs={{0,30},{1,31},{2,0},{3,1},{4,2},{5,3},{6,4},{7,5},{8,6},{9,7},{10,... | collective-permute-start | bytes 1544 | tf_op jit(solution)/shard_map/ppermute | solution.py:135
  10.7 5.7 %copy-start = (f32[2,1,2048]{2,1,0:T(1,128)S(1)}, f32[2,1,2048]{2,1,0:T(1,128)}, u32[]{:S(2)}) copy-start(f32[2,1,2048]{2,1,0:T(1,128)} %param.8) | copy-start | bytes 49156
  11.9 8.8 %collective-permute-start = (bf16[256,128]{1,0:T(8,128)(2,1)S(1)}, bf16[256,128]{1,0:T(8,128)(2,1)S(1)}, u32[]{:S(2)}, u32[]{:S(2)}) collective-permute-start(bf16[256,128]{1,0:T(8,128)(2,1)S(1)} %get-tuple-element.14), channel_id=1, source_target_pairs={{0,1},{1,0},{2,3},{3,2},{4,5},{5,4},{6,7},{7,6},{8,9},{9,8},{10,11... | collective-permute-start | bytes 196616 | tf_op jit(solution)/shard_map/ppermute | solution.py:135
  16.3 6.4 %collective-permute-start.4 = (bf16[256,128]{1,0:T(8,128)(2,1)S(1)}, bf16[256,128]{1,0:T(8,128)(2,1)S(1)}, u32[]{:S(2)}, u32[]{:S(2)}) collective-permute-start(bf16[256,128]{1,0:T(8,128)(2,1)S(1)} %get-tuple-element.15), channel_id=1, source_target_pairs={{0,2},{1,3},{2,4},{3,5},{4,6},{5,7},{6,8},{7,9},{8,10},{9,11},{10,... | collective-permute-start | bytes 196616 | tf_op jit(solution)/shard_map/ppermute | solution.py:135
  16.5 7.8 %collective-permute-start.5 = (bf16[256,128]{1,0:T(8,128)(2,1)S(1)}, bf16[256,128]{1,0:T(8,128)(2,1)S(1)}, u32[]{:S(2)}, u32[]{:S(2)}) collective-permute-start(bf16[256,128]{1,0:T(8,128)(2,1)S(1)} %get-tuple-element.16), channel_id=1, source_target_pairs={{0,3},{1,2},{2,5},{3,4},{4,7},{5,6},{6,9},{7,8},{8,11},{9,10},{10,... | collective-permute-start | bytes 196616 | tf_op jit(solution)/shard_map/ppermute | solution.py:135
  17.4 7.9 %collective-permute-start.6 = (bf16[256,128]{1,0:T(8,128)(2,1)S(1)}, bf16[256,128]{1,0:T(8,128)(2,1)S(1)}, u32[]{:S(2)}, u32[]{:S(2)}) collective-permute-start(bf16[256,128]{1,0:T(8,128)(2,1)S(1)} %get-tuple-element.17), channel_id=1, source_target_pairs={{0,4},{1,5},{2,6},{3,7},{4,8},{5,9},{6,10},{7,11},{8,12},{9,13},{1... | collective-permute-start | bytes 196616 | tf_op jit(solution)/shard_map/ppermute | solution.py:135
  19.8 8.6 %collective-permute-start.7 = (bf16[256,128]{1,0:T(8,128)(2,1)S(1)}, bf16[256,128]{1,0:T(8,128)(2,1)S(1)}, u32[]{:S(2)}, u32[]{:S(2)}) collective-permute-start(bf16[256,128]{1,0:T(8,128)(2,1)S(1)} %get-tuple-element.18), channel_id=1, source_target_pairs={{0,5},{1,4},{2,7},{3,6},{4,9},{5,8},{6,11},{7,10},{8,13},{9,12},{1... | collective-permute-start | bytes 196616 | tf_op jit(solution)/shard_map/ppermute | solution.py:135
  20.7 7.7 %collective-permute-start.8 = (bf16[256,128]{1,0:T(8,128)(2,1)S(1)}, bf16[256,128]{1,0:T(8,128)(2,1)S(1)}, u32[]{:S(2)}, u32[]{:S(2)}) collective-permute-start(bf16[256,128]{1,0:T(8,128)(2,1)S(1)} %get-tuple-element.19), channel_id=1, source_target_pairs={{0,6},{1,7},{2,8},{3,9},{4,10},{5,11},{6,12},{7,13},{8,14},{9,15},... | collective-permute-start | bytes 196616 | tf_op jit(solution)/shard_map/ppermute | solution.py:135
  22.7 6.4 %collective-permute-start.9 = (bf16[256,128]{1,0:T(8,128)(2,1)S(1)}, bf16[256,128]{1,0:T(8,128)(2,1)S(1)}, u32[]{:S(2)}, u32[]{:S(2)}) collective-permute-start(bf16[256,128]{1,0:T(8,128)(2,1)S(1)} %get-tuple-element.20), channel_id=1, source_target_pairs={{0,7},{1,6},{2,9},{3,8},{4,11},{5,10},{6,13},{7,12},{8,15},{9,14},... | collective-permute-start | bytes 196616 | tf_op jit(solution)/shard_map/ppermute | solution.py:135

commit v3 on v2

v3 whole, which is shorter than its diff:
```python
import functools
import math

import jax
import jax.numpy as jnp
import numpy as np
from jax import lax
from jax.experimental import pallas as pl
from jax.experimental.pallas import tpu as pltpu
from jax.sharding import PartitionSpec as P

ROW_DEV = 256
COL_DEV = 256
STEPS = 4
LANES = 128


def fitted(function, terms):
    nodes = np.cos(np.pi * (np.arange(64) + 0.5) / 64) * 0.25 + 0.25
    values = function(nodes)
    scale = np.vander(nodes * nodes, terms, increasing=True)
    return [float(c) for c in np.linalg.lstsq(scale, values, rcond=None)[0]]


COSINE = fitted(lambda x: np.cos(2 * np.pi * x), 9)
SINE = fitted(lambda x: np.sin(2 * np.pi * x) / x, 8)


def horner(coefficients, z):
    total = jnp.full_like(z, coefficients[-1])
    for c in coefficients[-2::-1]:
        total = total * z + c
    return total


NOTHING = pl.CostEstimate(flops=1, bytes_accessed=1, transcendentals=0)


def whole(space=pltpu.VMEM):
    return pl.BlockSpec(memory_space=space)


def block_twice(ref, row, block, width):
    per = LANES // width
    at = pl.multiple_of(block // per * LANES, LANES)
    line = ref[pl.ds(row, 1), pl.ds(at, LANES)]
    line = pltpu.roll(line, (LANES - block % per * width) % LANES, 1)
    lane = lax.broadcasted_iota(jnp.int32, line.shape, 1)
    return jnp.where(lane < width, line, pltpu.roll(line, width, 1))


def spread_kernel(pairs_ref, spread_ref):
    step = 256

    def one(k, carry):
        at = pl.multiple_of(k * step, step)
        spread_ref[pl.ds(at, step), :] = pairs_ref[pl.ds(at, step), :].astype(jnp.float32)
        return carry

    lax.fori_loop(0, pairs_ref.shape[0] // step, one, 0)


def table_kernel(tiles, groups, pulse_dev, steer_ref, table_ref, lines):
    columns = COL_DEV
    tile, group = lax.axis_index("tile"), lax.axis_index("pgroup")
    count = STEPS * groups
    odd = lax.rem(tile, 2)
    slots = [(0, f) for f in range(groups)]
    slots += [(back, f) for f in range(groups) for back in (2, 1 + 2 * odd)]
    slots += [(3 - 2 * odd, f) for f in range(groups)]
    for s, (back, f) in enumerate(slots):
        block = lax.rem(group + (groups - f), groups) * tiles + lax.rem(tile + (tiles - back), tiles)
        for row in range(2):
            at = 2 * s + row
            lines[at : at + 1, :] = block_twice(steer_ref, row, block, pulse_dev)
    upright = lines[...].T
    u = lax.broadcasted_iota(jnp.int32, (1, columns), 1).astype(jnp.float32)
    centred = u - (columns - 1) / 2.0
    linear = centred * (1.0 / (2 * math.pi))
    square = centred * centred * (1.0 / (2 * math.pi * columns))
    for s in range(count):
        rates = upright[:pulse_dev, 2 * s : 2 * s + 1]
        curves = upright[:pulse_dev, 2 * s + 1 : 2 * s + 2]
        turns = rates * linear + curves * square
        x = turns - jnp.round(turns)
        z = x * x
        cosine = horner(COSINE, z)
        sine = horner(SINE, z) * x
        c16 = cosine.astype(jnp.bfloat16)
        s16 = sine.astype(jnp.bfloat16)
        m16 = (-sine).astype(jnp.bfloat16)
        at = 2 * s * pulse_dev
        table_ref[at : at + pulse_dev, :columns] = c16
        table_ref[at : at + pulse_dev, columns:] = s16
        table_ref[at + pulse_dev : at + 2 * pulse_dev, :columns] = m16
        table_ref[at + pulse_dev : at + 2 * pulse_dev, columns:] = c16


def profile_kernel(pulse_dev, rows, range_rows, taps, phases, groups, count, *refs):
    scalars, vectors, echoes = refs[:count], refs[count : 2 * count], refs[2 * count : 3 * count]
    kern_ref, outs, (wide, tail, turned) = refs[3 * count], refs[3 * count + 1 : -3], refs[-3:]
    tall = 2 * rows // LANES
    lane = lax.broadcasted_iota(jnp.int32, (tall, LANES), 1)
    group = lax.axis_index("pgroup")

    for i in range(count):

        def align(p, carry, where=scalars[i], echo_ref=echoes[i]):
            first = where[0, p]
            row = 2 * (first >> 7)
            b = first & (LANES - 1)
            base = p * (2 * range_rows)
            x0 = echo_ref[pl.ds(base + row, tall), :]
            x1 = echo_ref[pl.ds(base + row + 2, tall), :]
            x2 = echo_ref[pl.ds(base + jnp.minimum(row + (tall - 4), 2 * range_rows - 8), 8), :]
            keep = lane >= b
            turn = LANES - b
            wide[pl.ds(pl.multiple_of(p * tall, 8), tall), :] = pltpu.roll(jnp.where(keep, x0, x1), turn, 1)
            end = jnp.where(keep[tall - 8 :], x1[tall - 8 :], x2)
            tail[pl.ds(pl.multiple_of(p * 8, 8), 8), :] = pltpu.roll(end, turn, 1)
            return carry

        lax.fori_loop(0, pulse_dev, align, 0, unroll=32)
        for r in range(rows // LANES):
            both = [wide[pl.ds(2 * r + q, pulse_dev, stride=tall), :] for q in range(2)]
            turned[r * LANES : (r + 1) * LANES, :] = jnp.concatenate(both, axis=0).T
        both = [tail[pl.ds(6 + q, pulse_dev, stride=8), :] for q in range(2)]
        turned[rows : rows + 8, :] = jnp.concatenate(both, axis=0).T[:8]

        phase = jnp.broadcast_to(vectors[i][1:2, :], (taps, 2 * pulse_dev))
        kern = kern_ref[0]
        for h in range(1, phases):
            kern = jnp.where(phase == h, kern_ref[h], kern)
        kern = [jnp.broadcast_to(kern[j : j + 1], (16, 2 * pulse_dev)) for j in range(taps)]
        for f in range(groups):
            base = lax.rem(group + f, groups) * ROW_DEV

            def fir(m, carry, out=outs[f], base=base, i=i):
                at = pl.multiple_of(m * 16, 16)
                summed = kern[0] * turned[pl.ds(base + at, 16), :]
                for j in range(1, taps):
                    summed = summed + kern[j] * turned[pl.ds(base + at + j, 16), :]
                out[pl.ds(at, 16), i * LANES : (i + 1) * LANES] = summed.astype(jnp.bfloat16)
                return carry

            lax.fori_loop(0, ROW_DEV // 16, fir, 0, unroll=4)


def project_kernel(count, normaliser, *refs):
    table_ref, out_ref = refs[count], refs[count + 1]
    left = jnp.concatenate([r[...] for r in refs[:count]], axis=1)
    image = jnp.dot(left, table_ref[...], preferred_element_type=jnp.float32)
    out_ref[0] = image[:, :COL_DEV] * normaliser
    out_ref[1] = image[:, COL_DEV:] * normaliser


def per_device(tiles, groups, echoes, offsets, phase_index, steering, kernels):
    pulse_dev, _, length = echoes.shape
    phases, taps = kernels.shape
    rows = ROW_DEV * groups
    range_rows = length // LANES
    tall = 2 * rows // LANES
    normaliser = (STEPS * pulse_dev * groups) ** (-0.5)
    params = pltpu.CompilerParams(vmem_limit_bytes=24 * 1024 * 1024)

    tile = lax.axis_index("tile")
    odd = tile % 2

    def sent(x, even_by, odd_by, flip):
        pairs = []
        for t in range(tiles):
            for g in range(groups):
                to = ((t + (odd_by if t % 2 else even_by)) % tiles) * groups + (g + flip) % groups
                pairs.append((t * groups + g, to))
        return lax.ppermute(x, ("tile", "pgroup"), pairs)

    def in_pairs(x):
        x = x.reshape(pulse_dev, 2, range_rows, LANES).transpose(0, 2, 1, 3)
        return x.reshape(pulse_dev * range_rows * 2, LANES)

    def spread(x):
        return pl.pallas_call(
            spread_kernel,
            out_shape=jax.ShapeDtypeStruct((pulse_dev * range_rows * 2, LANES), jnp.float32),
            in_specs=[whole()],
            out_specs=whole(),
            compiler_params=params,
            cost_estimate=NOTHING,
            name="spread",
        )(in_pairs(x))

    partner = sent(echoes, 1, -1, 0)
    mine = spread(echoes)
    theirs = spread(partner)
    kern = jnp.broadcast_to(kernels[:, :, None], (phases, taps, 2 * pulse_dev))

    both = jnp.concatenate([offsets, phase_index], axis=0)

    def where(block):
        piece = lax.dynamic_slice_in_dim(both, block % tiles * pulse_dev, pulse_dev, 1)
        return jnp.concatenate([piece, piece], axis=1)

    before = tile + tiles - 2
    ask = jnp.stack([where(before), where(before + 1 - 2 * odd)])
    far_ask = where(tile + tiles - 3 + 2 * odd)
    ask, far_ask = lax.optimization_barrier((sent(ask, -2, -2, 0), sent(far_ask, -3, -1, 0)))

    def profiles(wheres, sources):
        count = len(wheres)
        shape = jax.ShapeDtypeStruct((ROW_DEV, count * 2 * pulse_dev), jnp.bfloat16)
        return pl.pallas_call(
            functools.partial(profile_kernel, pulse_dev, rows, range_rows, taps, phases, groups, count),
            out_shape=[shape] * groups,
            in_specs=[whole(pltpu.SMEM)] * count + [whole()] * (2 * count + 1),
            out_specs=[whole()] * groups,
            scratch_shapes=[
                pltpu.VMEM((pulse_dev * tall, LANES), jnp.float32),
                pltpu.VMEM((pulse_dev * 8, LANES), jnp.float32),
                pltpu.VMEM((rows + 8, 2 * pulse_dev), jnp.float32),
            ],
            compiler_params=params,
            cost_estimate=NOTHING,
            name="profiles",
        )(*wheres, *wheres, *sources, kern)

    own = profiles([where(tile)], [mine])
    *own, ask, far_ask = lax.optimization_barrier((*own, ask, far_ask))
    own = [own[0]] + [sent(own[f], 0, 0, f) for f in range(1, groups)]
    near = profiles([ask[0], ask[1]], [mine, theirs])
    near = [sent(near[f], 2, 2, f) for f in range(groups)]
    far = profiles([far_ask], [mine])
    far = [sent(far[f], 1, 3, f) for f in range(groups)]

    count = STEPS * groups
    table = pl.pallas_call(
        functools.partial(table_kernel, tiles, groups, pulse_dev),
        out_shape=jax.ShapeDtypeStruct((2 * count * pulse_dev, 2 * COL_DEV), jnp.bfloat16),
        in_specs=[whole()],
        out_specs=whole(),
        scratch_shapes=[pltpu.VMEM((2 * count, LANES), jnp.float32)],
        compiler_params=params,
        cost_estimate=NOTHING,
        name="steering_table",
    )(steering[:, 0])

    left = own + near + far
    return pl.pallas_call(
        functools.partial(project_kernel, 3 * groups, normaliser),
        out_shape=jax.ShapeDtypeStruct((2, ROW_DEV, COL_DEV), jnp.float32),
        in_specs=[whole()] * (3 * groups + 1),
        out_specs=whole(),
        compiler_params=params,
        cost_estimate=NOTHING,
        name="project",
    )(*left, table)


def solution(mesh):
    placed = (
        P(("pgroup", "tile"), None, None),
        P("tile", "pgroup"),
        P("tile", "pgroup"),
        P(None, "tile", None),
        P(),
    )
    body = functools.partial(per_device, mesh.shape["tile"], mesh.shape["pgroup"])
    return jax.shard_map(body, mesh=mesh, in_specs=placed, out_specs=P(None, "pgroup", "tile"), check_vma=False)
```

time: 30.6 us -> 26.7 us (0.87)
  other arithmetic: 3.33 us -> 1.07 us
  starting transfers between devices: 13.2 us -> 11 us
  waiting for transfers between devices: 7.31 us -> 5.71 us
  Pallas kernels: 5.7 us -> 7.2 us
  local copies, waits for them, and re-layouts: 0.62 us -> 1.39 us
    ppermute x10 -> x8, starting transfers between devices: 13.2 us -> 11 us  [sent(): return lax.ppermute(x, ('tile', 'pgroup'), pairs)]
    reshape x1 -> x0, other arithmetic: 2.08 us -> none  [per_device(): spread = spread.reshape(pulse_dev * 2 * range_rows, LANES)]
    ppermute x10 -> x8, waiting for transfers between devices: 7.31 us -> 5.71 us  [sent(): return lax.ppermute(x, ('tile', 'pgroup'), pairs)]
    pallas_call x4 -> x7, Pallas kernels: 5.7 us -> 7.2 us  [the longest x3 4.51 us: profiles(): pl.pallas_call(functools.partial(profile_kernel, pulse_dev, rows, range_r...]
    unnamed x5 -> x8, local copies, waits for them, and re-layouts: 0.08 us -> 1.32 us
    concatenate x5 -> x3, other arithmetic: 1.16 us -> 0.99 us  [the longest x1 0.84 us: per_device(): both = jnp.concatenate([offsets, phase_index], axis=0)]
  transfers between devices with their start and end apart: 10 -> 8, of which waited for: 5 -> 3; matrix products, arithmetic and copies ran while one was open for 10% -> 5% of each run, Pallas kernels for 15% -> 14%
where the time goes in v3:
time: 26.7 us; the launch traced here: 26.5 us
  starting transfers between devices  11 us (41%)
  Pallas kernels  7.2 us (27%)
  waiting for transfers between devices  5.71 us (21%)
  local copies, waits for them, and re-layouts  1.39 us (5%)
  other arithmetic  1.07 us (4%)
    ppermute x8, starting transfers between devices, sent(): return lax.ppermute(x, ('tile', 'pgroup'), pairs)  11 us
    ppermute x8, waiting for transfers between devices, sent(): return lax.ppermute(x, ('tile', 'pgroup'), pairs)  5.71 us
    pallas_call x3, Pallas kernels, profiles(): pl.pallas_call(functools.partial(profile_kernel, pulse_dev, rows, range_r...  4.51 us
    unnamed x8, local copies, waits for them, and re-layouts  1.32 us
    pallas_call x1, Pallas kernels, per_device(): pl.pallas_call(functools.partial(project_kernel, 3 * groups, normaliser),...  1.23 us
    pallas_call x1, Pallas kernels, per_device(): pl.pallas_call(functools.partial(table_kernel, tiles, groups, pulse_dev),...  1.07 us
    concatenate x1, other arithmetic, per_device(): both = jnp.concatenate([offsets, phase_index], axis=0)  0.84 us
  transfers between devices with their start and end apart: 8, of which 3 were waited for; matrix products, arithmetic and copies ran while one was open for 5% of the time, Pallas kernels for 14%

profile of v3, /device:TPU:0, one launch (start us, length us, event | category | flops | bytes accessed | tf_op | source)
XLA Modules:
  0.0 26.5 jit_solution(1765710014830827270)
XLA Ops:
  0.0 0.5 %collective-permute-start.3 = (bf16[64,2,4096]{2,1,0:T(2,128)(2,1)}, bf16[64,2,4096]{2,1,0:T(2,128)(2,1)S(1)}, u32[]{:S(2)}, u32[]{:S(2)}) collective-permute-start(bf16[64,2,4096]{2,1,0:T(2,128)(2,1)} %param.5), channel_id=1, source_target_pairs={{0,2},{1,3},{2,0},{3,1},{4,6},{5,7},{6,4},{7,5},{8,10},{9,11},{10,... | collective-permute-start | bytes 3145736 | tf_op jit(solution)/shard_map/ppermute | solution.py:175
  0.5 0.8 %fusion = (s32[2,64]{1,0:T(2,128)S(1)}, s32[2,64]{1,0:T(2,128)S(1)}, s32[2,64]{1,0:T(2,128)S(1)}, s32[2,64]{1,0:T(2,128)S(1)}) fusion(s32[]{:T(128)S(6)} %select_n.43, s32[1,1024]{1,0:T(1,128)} %param.6, s32[1,1024]{1,0:T(1,128)} %param.7, s32[]{:T(128)S(6)} %select_n.36, s32[]{:T(128)S(6)} %select_n.38, s32[]{:T(128)S(6)} %select_n.41), kind=kLoop, calls=%fused_computation.10 | loop fusion | flops 512 | bytes 10256 | tf_op jit(solution)/shard_map/concatenate | solution.py:197
  1.3 0.1 add_bitcast_fusion
  1.4 5.6 %collective-permute-start = (s32[2,2,128]{2,1,0:T(2,128)S(1)}, s32[2,2,128]{2,1,0:T(2,128)S(1)}, u32[]{:S(2)}, u32[]{:S(2)}) collective-permute-start(s32[2,2,128]{2,1,0:T(2,128)S(1)} %pad_add_fusion), channel_id=1, source_target_pairs={{0,28},{1,29},{2,30},{3,31},{4,0},{5,1},{6,2},{7,3},{8,4},{9,5},{1... | collective-permute-start | bytes 6152 | tf_op jit(solution)/shard_map/ppermute | solution.py:175
  7.0 0.1 pad_add_fusion.2
  7.0 0.3 %collective-permute-start.1 = (s32[2,128]{1,0:T(2,128)S(1)}, s32[2,128]{1,0:T(2,128)S(1)}, u32[]{:S(2)}, u32[]{:S(2)}) collective-permute-start(s32[2,128]{1,0:T(2,128)S(1)} %pad_add_fusion.2), channel_id=1, source_target_pairs={{0,26},{1,27},{2,0},{3,1},{4,30},{5,31},{6,4},{7,5},{8,2},{9,3},{1... | collective-permute-start | bytes 3080 | tf_op jit(solution)/shard_map/ppermute | solution.py:175
  7.3 0.1 pad_add_fusion.1.refs_0_.refs_1_
  7.4 1.2 %copy-done = bf16[64,2,4096]{2,1,0:T(2,128)(2,1)S(1)} copy-done((bf16[64,2,4096]{2,1,0:T(2,128)(2,1)S(1)}, bf16[64,2,4096]{2,1,0:T(2,128)(2,1)}, u32[]{:S(2)}) %copy-start) | copy-done | bytes 1048600
  8.6 0.2 spread.2.refs_2_.refs_4_
  8.8 0.0 copy-done.2
  8.8 0.1 copy.7
  8.9 0.1 broadcast_in_dim.2.refs_3_.refs_6_
  9.0 1.3 %profiles.3 = (bf16[256,128]{1,0:T(8,128)(2,1)S(1)}, bf16[256,128]{1,0:T(8,128)(2,1)S(1)}) custom-call(s32[2,128]{1,0:T(2,128)S(1)} %pad_add_fusion.1.refs_0_.refs_1_, s32[2,128]{1,0:T(2,128)S(1)} %pad_add_fusion.1.refs_0_.refs_1_, f32[4096,128]{1,0:T(8,128)S(1)} %spread.2.refs_2_.refs_4_, f32[16,8,128]{2,1,0:T(8,128)S(1)} %broadcast_in_dim.2.refs_3_.refs_6_), custom_call_target="tpu_custom_call" | custom-call | flops 1 | bytes 1 | tf_op jit(solution)/shard_map/profiles/pallas_call | solution.py:211
  10.2 0.0 collective-permute-done.1.refs_0_.refs_1_
  10.2 0.0 collective-permute-done
  10.3 0.0 collective-permute-done.3
  10.3 0.2 spread.3.refs_5_
  10.5 2.0 %profiles.4 = (bf16[256,256]{1,0:T(8,128)(2,1)S(1)}, bf16[256,256]{1,0:T(8,128)(2,1)S(1)}) custom-call(s32[2,128]{1,0:T(2,128)S(1)} %get-tuple-element.34.refs_0_.refs_2_, s32[2,128]{1,0:T(2,128)S(1)} %get-tuple-element.33.refs_1_.refs_3_, s32[2,128]{1,0:T(2,128)S(1)} %get-tuple-element.34.refs_0_.refs_2_, s32[2,128]{1,0:T(2,128)S(1)} %get-tuple-element.33.refs_1_.refs_3_, ...), custom_call_target="tpu_custom_call" | custom-call | flops 1 | bytes 1 | tf_op jit(solution)/shard_map/profiles/pallas_call | solution.py:211
  12.5 0.0 copy-start.1
  12.5 0.7 %collective-permute-start.4 = (bf16[256,256]{1,0:T(8,128)(2,1)S(1)}, bf16[256,256]{1,0:T(8,128)(2,1)S(1)}, u32[]{:S(2)}, u32[]{:S(2)}) collective-permute-start(bf16[256,256]{1,0:T(8,128)(2,1)S(1)} %get-tuple-element.24), channel_id=1, source_target_pairs={{0,4},{1,5},{2,6},{3,7},{4,8},{5,9},{6,10},{7,11},{8,12},{9,13},{1... | collective-permute-start | bytes 393224 | tf_op jit(solution)/shard_map/ppermute | solution.py:175
  13.2 3.3 %collective-permute-start.5 = (bf16[256,256]{1,0:T(8,128)(2,1)S(1)}, bf16[256,256]{1,0:T(8,128)(2,1)S(1)}, u32[]{:S(2)}, u32[]{:S(2)}) collective-permute-start(bf16[256,256]{1,0:T(8,128)(2,1)S(1)} %get-tuple-element.25), channel_id=1, source_target_pairs={{0,5},{1,4},{2,7},{3,6},{4,9},{5,8},{6,11},{7,10},{8,13},{9,12},{1... | collective-permute-start | bytes 393224 | tf_op jit(solution)/shard_map/ppermute | solution.py:175
  16.5 1.3 %profiles.5 = (bf16[256,128]{1,0:T(8,128)(2,1)S(1)}, bf16[256,128]{1,0:T(8,128)(2,1)S(1)}) custom-call(s32[2,128]{1,0:T(2,128)S(1)} %collective-permute-done.1.refs_0_.refs_1_, s32[2,128]{1,0:T(2,128)S(1)} %collective-permute-done.1.refs_0_.refs_1_, f32[4096,128]{1,0:T(8,128)S(1)} %spread.2.refs_2_.refs_4_, f32[16,8,128]{2,1,0:T(8,128)S(1)} %broadcast_in_dim.2.refs_3_.refs_6_), custom_call_target="tpu_custom_call" | custom-call | flops 1 | bytes 1 | tf_op jit(solution)/shard_map/profiles/pallas_call | solution.py:211
  17.8 0.1 collective-permute-start.6
  17.8 0.1 collective-permute-start.7
  17.9 0.6 %collective-permute-start.2 = (bf16[256,128]{1,0:T(8,128)(2,1)S(1)}, bf16[256,128]{1,0:T(8,128)(2,1)S(1)}, u32[]{:S(2)}, u32[]{:S(2)}) collective-permute-start(bf16[256,128]{1,0:T(8,128)(2,1)S(1)} %get-tuple-element.22), channel_id=1, source_target_pairs={{0,1},{1,0},{2,3},{3,2},{4,5},{5,4},{6,7},{7,6},{8,9},{9,8},{10,11... | collective-permute-start | bytes 196616 | tf_op jit(solution)/shard_map/ppermute | solution.py:175
  18.5 1.1 %steering_table.1.refs_6_ = bf16[1024,512]{1,0:T(8,128)(2,1)S(1)} custom-call(f32[2,2048]{1,0:T(2,128)S(1)} %bitcast.23), custom_call_target="tpu_custom_call" | custom-call | flops 1 | bytes 1 | tf_op jit(solution)/shard_map/steering_table/pallas_call | solution.py:235
  19.6 3.7 %collective-permute-done.6.refs_4_ = bf16[256,128]{1,0:T(8,128)(2,1)S(1)} collective-permute-done((bf16[256,128]{1,0:T(8,128)(2,1)S(1)}, bf16[256,128]{1,0:T(8,128)(2,1)S(1)}, u32[]{:S(2)}, u32[]{:S(2)}) %collective-permute-start.6) | collective-permute-done | bytes 65568 | tf_op jit(solution)/shard_map/ppermute | solution.py:175
  23.3 1.0 %collective-permute-done.7.refs_5_ = bf16[256,128]{1,0:T(8,128)(2,1)S(1)} collective-permute-done((bf16[256,128]{1,0:T(8,128)(2,1)S(1)}, bf16[256,128]{1,0:T(8,128)(2,1)S(1)}, u32[]{:S(2)}, u32[]{:S(2)}) %collective-permute-start.7) | collective-permute-done | bytes 65568 | tf_op jit(solution)/shard_map/ppermute | solution.py:175
  24.3 0.0 collective-permute-done.2.refs_1_
  24.3 0.0 collective-permute-done.4.refs_2_
  24.3 1.0 %collective-permute-done.5.refs_3_ = bf16[256,256]{1,0:T(8,128)(2,1)S(1)} collective-permute-done((bf16[256,256]{1,0:T(8,128)(2,1)S(1)}, bf16[256,256]{1,0:T(8,128)(2,1)S(1)}, u32[]{:S(2)}, u32[]{:S(2)}) %collective-permute-start.5) | collective-permute-done | bytes 131104 | tf_op jit(solution)/shard_map/ppermute | solution.py:175
  25.3 1.2 %project.1 = f32[2,256,256]{2,1,0:T(8,128)} custom-call(bf16[256,128]{1,0:T(8,128)(2,1)S(1)} %get-tuple-element.21.refs_0_, bf16[256,128]{1,0:T(8,128)(2,1)S(1)} %collective-permute-done.2.refs_1_, bf16[256,256]{1,0:T(8,128)(2,1)S(1)} %collective-permute-done.4.refs_2_, bf16[256,256]{1,0:T(8,128)(2,1)S(1)} %collective-permute-done.5.refs_3_, ...), custom_call_target="tpu_custom_call" | custom-call | flops 1 | bytes 1 | tf_op jit(solution)/shard_map/project/pallas_call | solution.py:247
  (6 shorter events, 0.0 us)
Async XLA Ops:
  0.0 8.8 %copy-start.2 = (f32[16,8]{0,1:T(8,128)S(1)}, f32[16,8]{0,1:T(8,128)}, u32[]{:S(2)}) copy-start(f32[16,8]{0,1:T(8,128)} %param.9) | copy-start | bytes 1540
  0.0 10.3 %collective-permute-start.3 = (bf16[64,2,4096]{2,1,0:T(2,128)(2,1)}, bf16[64,2,4096]{2,1,0:T(2,128)(2,1)S(1)}, u32[]{:S(2)}, u32[]{:S(2)}) collective-permute-start(bf16[64,2,4096]{2,1,0:T(2,128)(2,1)} %param.5), channel_id=1, source_target_pairs={{0,2},{1,3},{2,0},{3,1},{4,6},{5,7},{6,4},{7,5},{8,10},{9,11},{10,... | collective-permute-start | bytes 3145736 | tf_op jit(solution)/shard_map/ppermute | solution.py:175
  1.4 8.9 %collective-permute-start = (s32[2,2,128]{2,1,0:T(2,128)S(1)}, s32[2,2,128]{2,1,0:T(2,128)S(1)}, u32[]{:S(2)}, u32[]{:S(2)}) collective-permute-start(s32[2,2,128]{2,1,0:T(2,128)S(1)} %pad_add_fusion), channel_id=1, source_target_pairs={{0,28},{1,29},{2,30},{3,31},{4,0},{5,1},{6,2},{7,3},{8,4},{9,5},{1... | collective-permute-start | bytes 6152 | tf_op jit(solution)/shard_map/ppermute | solution.py:175
  7.0 3.2 %collective-permute-start.1 = (s32[2,128]{1,0:T(2,128)S(1)}, s32[2,128]{1,0:T(2,128)S(1)}, u32[]{:S(2)}, u32[]{:S(2)}) collective-permute-start(s32[2,128]{1,0:T(2,128)S(1)} %pad_add_fusion.2), channel_id=1, source_target_pairs={{0,26},{1,27},{2,0},{3,1},{4,30},{5,31},{6,4},{7,5},{8,2},{9,3},{1... | collective-permute-start | bytes 3080 | tf_op jit(solution)/shard_map/ppermute | solution.py:175
  7.4 1.2 %copy-start = (bf16[64,2,4096]{2,1,0:T(2,128)(2,1)S(1)}, bf16[64,2,4096]{2,1,0:T(2,128)(2,1)}, u32[]{:S(2)}) copy-start(bf16[64,2,4096]{2,1,0:T(2,128)(2,1)} %param.5) | copy-start | bytes 3145732
  12.5 6.0 %copy-start.1 = (f32[2,1,2048]{2,1,0:T(1,128)S(1)}, f32[2,1,2048]{2,1,0:T(1,128)}, u32[]{:S(2)}) copy-start(f32[2,1,2048]{2,1,0:T(1,128)} %param.8) | copy-start | bytes 49156
  12.5 11.8 %collective-permute-start.4 = (bf16[256,256]{1,0:T(8,128)(2,1)S(1)}, bf16[256,256]{1,0:T(8,128)(2,1)S(1)}, u32[]{:S(2)}, u32[]{:S(2)}) collective-permute-start(bf16[256,256]{1,0:T(8,128)(2,1)S(1)} %get-tuple-element.24), channel_id=1, source_target_pairs={{0,4},{1,5},{2,6},{3,7},{4,8},{5,9},{6,10},{7,11},{8,12},{9,13},{1... | collective-permute-start | bytes 393224 | tf_op jit(solution)/shard_map/ppermute | solution.py:175
  13.2 12.1 %collective-permute-start.5 = (bf16[256,256]{1,0:T(8,128)(2,1)S(1)}, bf16[256,256]{1,0:T(8,128)(2,1)S(1)}, u32[]{:S(2)}, u32[]{:S(2)}) collective-permute-start(bf16[256,256]{1,0:T(8,128)(2,1)S(1)} %get-tuple-element.25), channel_id=1, source_target_pairs={{0,5},{1,4},{2,7},{3,6},{4,9},{5,8},{6,11},{7,10},{8,13},{9,12},{1... | collective-permute-start | bytes 393224 | tf_op jit(solution)/shard_map/ppermute | solution.py:175
  17.8 5.5 %collective-permute-start.6 = (bf16[256,128]{1,0:T(8,128)(2,1)S(1)}, bf16[256,128]{1,0:T(8,128)(2,1)S(1)}, u32[]{:S(2)}, u32[]{:S(2)}) collective-permute-start(bf16[256,128]{1,0:T(8,128)(2,1)S(1)} %get-tuple-element.27), channel_id=1, source_target_pairs={{0,2},{1,3},{2,8},{3,9},{4,6},{5,7},{6,12},{7,13},{8,10},{9,11},{1... | collective-permute-start | bytes 196616 | tf_op jit(solution)/shard_map/ppermute | solution.py:175
  17.8 6.4 %collective-permute-start.7 = (bf16[256,128]{1,0:T(8,128)(2,1)S(1)}, bf16[256,128]{1,0:T(8,128)(2,1)S(1)}, u32[]{:S(2)}, u32[]{:S(2)}) collective-permute-start(bf16[256,128]{1,0:T(8,128)(2,1)S(1)} %get-tuple-element.28), channel_id=1, source_target_pairs={{0,3},{1,2},{2,9},{3,8},{4,7},{5,6},{6,13},{7,12},{8,11},{9,10},{1... | collective-permute-start | bytes 196616 | tf_op jit(solution)/shard_map/ppermute | solution.py:175
  17.9 6.4 %collective-permute-start.2 = (bf16[256,128]{1,0:T(8,128)(2,1)S(1)}, bf16[256,128]{1,0:T(8,128)(2,1)S(1)}, u32[]{:S(2)}, u32[]{:S(2)}) collective-permute-start(bf16[256,128]{1,0:T(8,128)(2,1)S(1)} %get-tuple-element.22), channel_id=1, source_target_pairs={{0,1},{1,0},{2,3},{3,2},{4,5},{5,4},{6,7},{7,6},{8,9},{9,8},{10,11... | collective-permute-start | bytes 196616 | tf_op jit(solution)/shard_map/ppermute | solution.py:175

commit v4 on v3

--- a/solution.py
+++ b/solution.py
@@ -50,14 +50,7 @@
 
 
 def spread_kernel(pairs_ref, spread_ref):
-    step = 256
-
-    def one(k, carry):
-        at = pl.multiple_of(k * step, step)
-        spread_ref[pl.ds(at, step), :] = pairs_ref[pl.ds(at, step), :].astype(jnp.float32)
-        return carry
-
-    lax.fori_loop(0, pairs_ref.shape[0] // step, one, 0)
+    spread_rows(pairs_ref, spread_ref)
 
 
 def table_kernel(tiles, groups, pulse_dev, steer_ref, table_ref, lines):
@@ -66,8 +59,8 @@
     count = STEPS * groups
     odd = lax.rem(tile, 2)
     slots = [(0, f) for f in range(groups)]
+    slots += [(3 - 2 * odd, f) for f in range(groups)]
     slots += [(back, f) for f in range(groups) for back in (2, 1 + 2 * odd)]
-    slots += [(3 - 2 * odd, f) for f in range(groups)]
     for s, (back, f) in enumerate(slots):
         block = lax.rem(group + (groups - f), groups) * tiles + lax.rem(tile + (tiles - back), tiles)
         for row in range(2):
@@ -96,62 +89,86 @@
         table_ref[at + pulse_dev : at + 2 * pulse_dev, columns:] = c16
 
 
-def profile_kernel(pulse_dev, rows, range_rows, taps, phases, groups, count, *refs):
-    scalars, vectors, echoes = refs[:count], refs[count : 2 * count], refs[2 * count : 3 * count]
-    kern_ref, outs, (wide, tail, turned) = refs[3 * count], refs[3 * count + 1 : -3], refs[-3:]
+def spread_rows(pairs_ref, spread_ref):
+    step = 256
+
+    def one(k, carry):
+        at = pl.multiple_of(k * step, step)
+        spread_ref[pl.ds(at, step), :] = pairs_ref[pl.ds(at, step), :].astype(jnp.float32)
+        return carry
+
+    lax.fori_loop(0, pairs_ref.shape[0] // step, one, 0)
+
+
+def profile_kernel(pulse_dev, rows, taps, phases, groups, raw, joined, *refs):
+    count = len(raw)
+    asks, kern_ref, refs = refs[:count], refs[count], refs[count + 1 :]
+    echoes, refs = list(refs[:count]), refs[count:]
+    outs, (wide, tail, turned, scalars, sems, *spare) = refs[: groups * (1 if joined else count)], refs[-5 - sum(raw) :]
+    copies = [pltpu.make_async_copy(asks[i], scalars.at[i], sems.at[i]) for i in range(count)]
+    for copy in copies:
+        copy.start()
     tall = 2 * rows // LANES
     lane = lax.broadcasted_iota(jnp.int32, (tall, LANES), 1)
     group = lax.axis_index("pgroup")
-
+    kerns = []
     for i in range(count):
-
-        def align(p, carry, where=scalars[i], echo_ref=echoes[i]):
-            first = where[0, p]
-            row = 2 * (first >> 7)
-            b = first & (LANES - 1)
-            base = p * (2 * range_rows)
-            x0 = echo_ref[pl.ds(base + row, tall), :]
-            x1 = echo_ref[pl.ds(base + row + 2, tall), :]
-            x2 = echo_ref[pl.ds(base + jnp.minimum(row + (tall - 4), 2 * range_rows - 8), 8), :]
+        phase = jnp.broadcast_to(asks[i][3:4, :], (taps, 2 * pulse_dev))
+        kern = kern_ref[0]
+        for h in range(1, phases):
+            kern = jnp.where(phase == h, kern_ref[h], kern)
+        kerns.append(kern)
+        if raw[i]:
+            spread_rows(echoes[i], spare[0])
+            echoes[i] = spare[0]
+
+    for i in range(count):
+        copies[i].wait()
+        for p in range(pulse_dev):
+            first, last, b = scalars[i, 0, p], scalars[i, 1, p], scalars[i, 2, p]
+            x0 = echoes[i][pl.ds(first, tall), :]
+            x1 = echoes[i][pl.ds(first + 2, tall), :]
+            x2 = echoes[i][pl.ds(last, 8), :]
             keep = lane >= b
             turn = LANES - b
-            wide[pl.ds(pl.multiple_of(p * tall, 8), tall), :] = pltpu.roll(jnp.where(keep, x0, x1), turn, 1)
+            wide[p * tall : (p + 1) * tall, :] = pltpu.roll(jnp.where(keep, x0, x1), turn, 1)
             end = jnp.where(keep[tall - 8 :], x1[tall - 8 :], x2)
-            tail[pl.ds(pl.multiple_of(p * 8, 8), 8), :] = pltpu.roll(end, turn, 1)
-            return carry
-
-        lax.fori_loop(0, pulse_dev, align, 0, unroll=32)
+            tail[p * 8 : (p + 1) * 8, :] = pltpu.roll(end, turn, 1)
         for r in range(rows // LANES):
             both = [wide[pl.ds(2 * r + q, pulse_dev, stride=tall), :] for q in range(2)]
             turned[r * LANES : (r + 1) * LANES, :] = jnp.concatenate(both, axis=0).T
         both = [tail[pl.ds(6 + q, pulse_dev, stride=8), :] for q in range(2)]
         turned[rows : rows + 8, :] = jnp.concatenate(both, axis=0).T[:8]
 
-        phase = jnp.broadcast_to(vectors[i][1:2, :], (taps, 2 * pulse_dev))
-        kern = kern_ref[0]
-        for h in range(1, phases):
-            kern = jnp.where(phase == h, kern_ref[h], kern)
-        kern = [jnp.broadcast_to(kern[j : j + 1], (16, 2 * pulse_dev)) for j in range(taps)]
+        kern = [jnp.broadcast_to(kerns[i][j : j + 1], (16, 2 * pulse_dev)) for j in range(taps)]
         for f in range(groups):
             base = lax.rem(group + f, groups) * ROW_DEV
-
-            def fir(m, carry, out=outs[f], base=base, i=i):
+            out = outs[f if joined else i * groups + f]
+            lanes = slice(i * LANES, (i + 1) * LANES) if joined else slice(0, LANES)
+
+            def fir(m, carry, out=out, lanes=lanes, base=base):
                 at = pl.multiple_of(m * 16, 16)
                 summed = kern[0] * turned[pl.ds(base + at, 16), :]
                 for j in range(1, taps):
                     summed = summed + kern[j] * turned[pl.ds(base + at + j, 16), :]
-                out[pl.ds(at, 16), i * LANES : (i + 1) * LANES] = summed.astype(jnp.bfloat16)
+                out[pl.ds(at, 16), lanes] = summed.astype(jnp.bfloat16)
                 return carry
 
             lax.fori_loop(0, ROW_DEV // 16, fir, 0, unroll=4)
 
 
-def project_kernel(count, normaliser, *refs):
-    table_ref, out_ref = refs[count], refs[count + 1]
-    left = jnp.concatenate([r[...] for r in refs[:count]], axis=1)
-    image = jnp.dot(left, table_ref[...], preferred_element_type=jnp.float32)
-    out_ref[0] = image[:, :COL_DEV] * normaliser
-    out_ref[1] = image[:, COL_DEV:] * normaliser
+def project_kernel(count, first, normaliser, *refs):
+    pieces, table_ref, out_ref = refs[:count], refs[count], refs[-1]
+    left = jnp.concatenate([r[...] for r in pieces], axis=1)
+    rows = table_ref[first : first + left.shape[1], :]
+    image = jnp.dot(left, rows, preferred_element_type=jnp.float32)
+    if len(refs) > count + 2:
+        image = image + refs[count + 1][...]
+    if normaliser is None:
+        out_ref[...] = image
+    else:
+        out_ref[0] = image[:, :COL_DEV] * normaliser
+        out_ref[1] = image[:, COL_DEV:] * normaliser
 
 
 def per_device(tiles, groups, echoes, offsets, phase_index, steering, kernels):
@@ -191,45 +208,53 @@
 
     partner = sent(echoes, 1, -1, 0)
     mine = spread(echoes)
-    theirs = spread(partner)
+    theirs = in_pairs(partner)
     kern = jnp.broadcast_to(kernels[:, :, None], (phases, taps, 2 * pulse_dev))
 
     both = jnp.concatenate([offsets, phase_index], axis=0)
 
-    def where(block):
-        piece = lax.dynamic_slice_in_dim(both, block % tiles * pulse_dev, pulse_dev, 1)
-        return jnp.concatenate([piece, piece], axis=1)
+    def block_of(block):
+        return lax.dynamic_slice_in_dim(both, block % tiles * pulse_dev, pulse_dev, 1)
 
     before = tile + tiles - 2
-    ask = jnp.stack([where(before), where(before + 1 - 2 * odd)])
-    far_ask = where(tile + tiles - 3 + 2 * odd)
-    ask, far_ask = lax.optimization_barrier((sent(ask, -2, -2, 0), sent(far_ask, -3, -1, 0)))
-
-    def profiles(wheres, sources):
-        count = len(wheres)
-        shape = jax.ShapeDtypeStruct((ROW_DEV, count * 2 * pulse_dev), jnp.bfloat16)
+    blocks = [before, before + 1 - 2 * odd, tile + tiles - 3 + 2 * odd, tile]
+    told = jnp.stack([block_of(block) for block in blocks])
+    row = 2 * (told[:, :1] // LANES)
+    base = 2 * range_rows * jnp.arange(pulse_dev, dtype=jnp.int32)
+    last = jnp.minimum(row + (tall - 4), 2 * range_rows - 8)
+    told = jnp.concatenate([base + row, base + last, told[:, :1] % LANES, told[:, 1:]], axis=1)
+    told = jnp.concatenate([told, told], axis=2)
+    far_ask = sent(told[2], -3, -1, 0)
+    ask = sent(told[:2], -2, -2, 0)
+    far_ask, ask = lax.optimization_barrier((far_ask, ask))
+
+    def profiles(asks, sources, raw, joined):
+        count = len(sources)
+        shape = jax.ShapeDtypeStruct((ROW_DEV, (count if joined else 1) * 2 * pulse_dev), jnp.bfloat16)
+        outs = groups * (1 if joined else count)
         return pl.pallas_call(
-            functools.partial(profile_kernel, pulse_dev, rows, range_rows, taps, phases, groups, count),
-            out_shape=[shape] * groups,
-            in_specs=[whole(pltpu.SMEM)] * count + [whole()] * (2 * count + 1),
-            out_specs=[whole()] * groups,
+            functools.partial(profile_kernel, pulse_dev, rows, taps, phases, groups, raw, joined),
+            out_shape=[shape] * outs,
+            in_specs=[whole()] * (2 * count + 1),
+            out_specs=[whole()] * outs,
             scratch_shapes=[
                 pltpu.VMEM((pulse_dev * tall, LANES), jnp.float32),
                 pltpu.VMEM((pulse_dev * 8, LANES), jnp.float32),
                 pltpu.VMEM((rows + 8, 2 * pulse_dev), jnp.float32),
-            ],
+                pltpu.SMEM((count, 4, 2 * pulse_dev), jnp.int32),
+                pltpu.SemaphoreType.DMA((count,)),
+            ]
+            + [pltpu.VMEM((pulse_dev * 2 * range_rows, LANES), jnp.float32)] * sum(raw),
             compiler_params=params,
             cost_estimate=NOTHING,
             name="profiles",
-        )(*wheres, *wheres, *sources, kern)
-
-    own = profiles([where(tile)], [mine])
-    *own, ask, far_ask = lax.optimization_barrier((*own, ask, far_ask))
-    own = [own[0]] + [sent(own[f], 0, 0, f) for f in range(1, groups)]
-    near = profiles([ask[0], ask[1]], [mine, theirs])
+        )(*asks, kern, *sources)
+
+    near = profiles([ask[0], ask[1]], [mine, theirs], (False, True), True)
     near = [sent(near[f], 2, 2, f) for f in range(groups)]
-    far = profiles([far_ask], [mine])
-    far = [sent(far[f], 1, 3, f) for f in range(groups)]
+    rest = profiles([far_ask, told[3]], [mine, mine], (False, False), False)
+    far = [sent(rest[f], 1, 3, f) for f in range(groups)]
+    own = [rest[groups]] + [sent(rest[groups + f], 0, 0, f) for f in range(1, groups)]
 
     count = STEPS * groups
     table = pl.pallas_call(
@@ -243,16 +268,22 @@
         name="steering_table",
     )(steering[:, 0])
 
-    left = own + near + far
-    return pl.pallas_call(
-        functools.partial(project_kernel, 3 * groups, normaliser),
-        out_shape=jax.ShapeDtypeStruct((2, ROW_DEV, COL_DEV), jnp.float32),
-        in_specs=[whole()] * (3 * groups + 1),
-        out_specs=whole(),
-        compiler_params=params,
-        cost_estimate=NOTHING,
-        name="project",
-    )(*left, table)
+    def project(pieces, first, total, last):
+        shape = (2, ROW_DEV, COL_DEV) if last else (ROW_DEV, 2 * COL_DEV)
+        given = list(pieces) + [table] + ([] if total is None else [total])
+        return pl.pallas_call(
+            functools.partial(project_kernel, len(pieces), first, normaliser if last else None),
+            out_shape=jax.ShapeDtypeStruct(shape, jnp.float32),
+            in_specs=[whole()] * len(given),
+            out_specs=whole(),
+            compiler_params=params,
+            cost_estimate=NOTHING,
+            name="project",
+        )(*given)
+
+    wide = 2 * pulse_dev
+    total = project(near, 2 * groups * wide, None, False)
+    return project(own + far, 0, total, True)
 
 
 def solution(mesh):

time: 26.7 us -> 25.4 us (0.951)
  Pallas kernels: 7.2 us -> 6 us
    pallas_call x4, Pallas kernels: 5.74 us -> 4.75 us  [the longest x2 3.36 us: profiles(): pl.pallas_call(functools.partial(profile_kernel, pulse_dev, rows, taps, p...]
    concatenate x3 -> x1, other arithmetic: 0.99 us -> 0.09 us  [per_device(): told = jnp.concatenate([told, told], axis=2)]
    another operation x2, other arithmetic: 0.08 us -> 0.85 us  [per_device(): told = jnp.stack([block_of(block) for block in blocks])]
  transfers between devices with their start and end apart: 8 -> 8, of which waited for: 3 -> 3; matrix products, arithmetic and copies ran while one was open for 5% -> 5% of each run, Pallas kernels for 14% -> 13%
where the time goes in v4:
time: 25.4 us; the launch traced here: 25.3 us
  starting transfers between devices  11 us (43%)
  Pallas kernels  6 us (24%)
  waiting for transfers between devices  5.69 us (22%)
  local copies, waits for them, and re-layouts  1.4 us (6%)
  other arithmetic  1.05 us (4%)
    ppermute x8, starting transfers between devices, sent(): return lax.ppermute(x, ('tile', 'pgroup'), pairs)  11 us
    ppermute x8, waiting for transfers between devices, sent(): return lax.ppermute(x, ('tile', 'pgroup'), pairs)  5.69 us
    pallas_call x2, Pallas kernels, profiles(): pl.pallas_call(functools.partial(profile_kernel, pulse_dev, rows, taps, p...  3.36 us
    pallas_call x2, Pallas kernels, project(): pl.pallas_call(functools.partial(project_kernel, len(pieces), first, norm...  1.39 us
    unnamed x8, local copies, waits for them, and re-layouts  1.31 us
    pallas_call x1, Pallas kernels, per_device(): pl.pallas_call(functools.partial(table_kernel, tiles, groups, pulse_dev),...  1.07 us
    another operation x2, other arithmetic, per_device(): told = jnp.stack([block_of(block) for block in blocks])  0.85 us
  transfers between devices with their start and end apart: 8, of which 3 were waited for; matrix products, arithmetic and copies ran while one was open for 5% of the time, Pallas kernels for 13%

profile of v4, /device:TPU:0, one launch (start us, length us, event | category | flops | bytes accessed | tf_op | source)
XLA Modules:
  0.0 25.3 jit_solution(12486833966494034943)
XLA Ops:
  0.0 0.0 copy-start.2
  0.0 0.5 %collective-permute-start.5 = (bf16[64,2,4096]{2,1,0:T(2,128)(2,1)}, bf16[64,2,4096]{2,1,0:T(2,128)(2,1)S(1)}, u32[]{:S(2)}, u32[]{:S(2)}) collective-permute-start(bf16[64,2,4096]{2,1,0:T(2,128)(2,1)} %param.5), channel_id=1, source_target_pairs={{0,2},{1,3},{2,0},{3,1},{4,6},{5,7},{6,4},{7,5},{8,10},{9,11},{10,... | collective-permute-start | bytes 3145736 | tf_op jit(solution)/shard_map/ppermute | solution.py:192
  0.5 0.8 %fusion.7 = (s32[1,2,64]{2,1,0:T(2,128)S(1)}, s32[1,2,64]{2,1,0:T(2,128)S(1)}, s32[1,2,64]{2,1,0:T(2,128)S(1)}, s32[1,2,64]{2,1,0:T(2,128)S(1)}) fusion(s32[]{:T(128)S(6)} %select_n.47, s32[1,1024]{1,0:T(1,128)} %param.7, s32[1,1024]{1,0:T(1,128)} %param.6, s32[]{:T(128)S(6)} %select_n.50, s32[]{:T(128)S(6)} %select_n.52, s32[]{:T(128)S(6)} %select_n.54), kind=kLoop, calls=%fused_computation.28 | loop fusion | flops 512 | bytes 10256 | tf_op jit(solution)/shard_map/stack | solution.py:221
  1.4 0.1 add_add_fusion
  1.5 5.6 %collective-permute-start.1 = (s32[2,4,128]{2,1,0:T(4,128)S(1)}, s32[2,4,128]{2,1,0:T(4,128)S(1)}, u32[]{:S(2)}, u32[]{:S(2)}) collective-permute-start(s32[2,4,128]{2,1,0:T(4,128)S(1)} %slice.31), channel_id=1, source_target_pairs={{0,28},{1,29},{2,30},{3,31},{4,0},{5,1},{6,2},{7,3},{8,4},{9,5},{1... | collective-permute-start | bytes 12296 | tf_op jit(solution)/shard_map/ppermute | solution.py:192
  7.1 0.1 add_bitcast_fusion
  7.2 0.3 %collective-permute-start = (s32[4,128]{1,0:T(4,128)S(1)}, s32[4,128]{1,0:T(4,128)S(1)}, u32[]{:S(2)}, u32[]{:S(2)}) collective-permute-start(s32[4,128]{1,0:T(4,128)S(1)} %get-tuple-element.25), channel_id=1, source_target_pairs={{0,26},{1,27},{2,0},{3,1},{4,30},{5,31},{6,4},{7,5},{8,2},{9,3},{1... | collective-permute-start | bytes 6152 | tf_op jit(solution)/shard_map/ppermute | solution.py:192
  7.4 0.0 copy-start
  7.4 1.2 %copy-done = bf16[64,2,4096]{2,1,0:T(2,128)(2,1)S(1)} copy-done((bf16[64,2,4096]{2,1,0:T(2,128)(2,1)S(1)}, bf16[64,2,4096]{2,1,0:T(2,128)(2,1)}, u32[]{:S(2)}) %copy-start) | copy-done | bytes 1048600
  8.7 0.2 spread.1.refs_3_.refs_4_
  8.9 0.0 copy-done.2
  8.9 0.1 copy.11
  8.9 0.0 collective-permute-done.refs_0_
  8.9 0.0 collective-permute-done.1
  9.0 0.0 collective-permute-done.5
  9.0 0.1 broadcast_in_dim.2.refs_2_
  9.0 1.7 %profiles.3 = (bf16[256,256]{1,0:T(8,128)(2,1)S(1)}, bf16[256,256]{1,0:T(8,128)(2,1)S(1)}) custom-call(s32[4,128]{1,0:T(4,128)S(1)} %get-tuple-element.31.refs_0_, s32[4,128]{1,0:T(4,128)S(1)} %get-tuple-element.30.refs_1_, f32[16,8,128]{2,1,0:T(8,128)S(1)} %broadcast_in_dim.2.refs_2_, f32[4096,128]{1,0:T(8,128)S(1)} %spread.1.refs_3_.refs_4_, ...), custom_call_target="tpu_custom_call" | custom-call | flops 1 | bytes 1 | tf_op jit(solution)/shard_map/profiles/pallas_call | solution.py:235
  10.7 0.7 %collective-permute-start.6 = (bf16[256,256]{1,0:T(8,128)(2,1)S(1)}, bf16[256,256]{1,0:T(8,128)(2,1)S(1)}, u32[]{:S(2)}, u32[]{:S(2)}) collective-permute-start(bf16[256,256]{1,0:T(8,128)(2,1)S(1)} %get-tuple-element.19), channel_id=1, source_target_pairs={{0,4},{1,5},{2,6},{3,7},{4,8},{5,9},{6,10},{7,11},{8,12},{9,13},{1... | collective-permute-start | bytes 393224 | tf_op jit(solution)/shard_map/ppermute | solution.py:192
  11.4 3.3 %collective-permute-start.7 = (bf16[256,256]{1,0:T(8,128)(2,1)S(1)}, bf16[256,256]{1,0:T(8,128)(2,1)S(1)}, u32[]{:S(2)}, u32[]{:S(2)}) collective-permute-start(bf16[256,256]{1,0:T(8,128)(2,1)S(1)} %get-tuple-element.20), channel_id=1, source_target_pairs={{0,5},{1,4},{2,7},{3,6},{4,9},{5,8},{6,11},{7,10},{8,13},{9,12},{1... | collective-permute-start | bytes 393224 | tf_op jit(solution)/shard_map/ppermute | solution.py:192
  14.8 1.7 %profiles.2 = (bf16[256,128]{1,0:T(8,128)(2,1)S(1)}, bf16[256,128]{1,0:T(8,128)(2,1)S(1)}, bf16[256,128]{1,0:T(8,128)(2,1)S(1)}, bf16[256,128]{1,0:T(8,128)(2,1)S(1)}) custom-call(s32[4,128]{1,0:T(4,128)S(1)} %collective-permute-done.refs_0_, s32[4,128]{1,0:T(4,128)S(1)} %get-tuple-element.24.refs_1_, f32[16,8,128]{2,1,0:T(8,128)S(1)} %broadcast_in_dim.2.refs_2_, ...), custom_call_target="tpu_custom_call" | custom-call | flops 1 | bytes 1 | tf_op jit(solution)/shard_map/profiles/pallas_call | solution.py:235
  16.4 0.6 %collective-permute-start.2 = (bf16[256,128]{1,0:T(8,128)(2,1)S(1)}, bf16[256,128]{1,0:T(8,128)(2,1)S(1)}, u32[]{:S(2)}, u32[]{:S(2)}) collective-permute-start(bf16[256,128]{1,0:T(8,128)(2,1)S(1)} %get-tuple-element.15), channel_id=1, source_target_pairs={{0,1},{1,0},{2,3},{3,2},{4,5},{5,4},{6,7},{7,6},{8,9},{9,8},{10,11... | collective-permute-start | bytes 196616 | tf_op jit(solution)/shard_map/ppermute | solution.py:192
  17.1 0.0 collective-permute-start.3
  17.1 0.0 collective-permute-start.4
  17.1 0.0 copy-done.1
  17.1 1.1 %steering_table.1.refs_2_.refs_4_ = bf16[1024,512]{1,0:T(8,128)(2,1)S(1)} custom-call(f32[2,2048]{1,0:T(2,128)S(1)} %bitcast.32), custom_call_target="tpu_custom_call" | custom-call | flops 1 | bytes 1 | tf_op jit(solution)/shard_map/steering_table/pallas_call | solution.py:260
  18.2 1.3 %collective-permute-done.6.refs_0_ = bf16[256,256]{1,0:T(8,128)(2,1)S(1)} collective-permute-done((bf16[256,256]{1,0:T(8,128)(2,1)S(1)}, bf16[256,256]{1,0:T(8,128)(2,1)S(1)}, u32[]{:S(2)}, u32[]{:S(2)}) %collective-permute-start.6) | collective-permute-done | bytes 131104 | tf_op jit(solution)/shard_map/ppermute | solution.py:192
  19.5 3.8 %collective-permute-done.7.refs_1_ = bf16[256,256]{1,0:T(8,128)(2,1)S(1)} collective-permute-done((bf16[256,256]{1,0:T(8,128)(2,1)S(1)}, bf16[256,256]{1,0:T(8,128)(2,1)S(1)}, u32[]{:S(2)}, u32[]{:S(2)}) %collective-permute-start.7) | collective-permute-done | bytes 131104 | tf_op jit(solution)/shard_map/ppermute | solution.py:192
  23.3 0.3 %project.2.refs_5_ = f32[256,512]{1,0:T(8,128)S(1)} custom-call(bf16[256,256]{1,0:T(8,128)(2,1)S(1)} %collective-permute-done.6.refs_0_, bf16[256,256]{1,0:T(8,128)(2,1)S(1)} %collective-permute-done.7.refs_1_, bf16[1024,512]{1,0:T(8,128)(2,1)S(1)} %steering_table.1.refs_2_.refs_4_), custom_call_target="tpu_custom_call" | custom-call | flops 1 | bytes 1 | tf_op jit(solution)/shard_map/project/pallas_call | solution.py:274
  23.6 0.0 collective-permute-done.2.refs_1_
  23.6 0.0 collective-permute-done.3.refs_2_
  23.6 0.5 %collective-permute-done.4.refs_3_ = bf16[256,128]{1,0:T(8,128)(2,1)S(1)} collective-permute-done((bf16[256,128]{1,0:T(8,128)(2,1)S(1)}, bf16[256,128]{1,0:T(8,128)(2,1)S(1)}, u32[]{:S(2)}, u32[]{:S(2)}) %collective-permute-start.4) | collective-permute-done | bytes 65568 | tf_op jit(solution)/shard_map/ppermute | solution.py:192
  24.2 1.1 %project.3 = f32[2,256,256]{2,1,0:T(8,128)} custom-call(bf16[256,128]{1,0:T(8,128)(2,1)S(1)} %get-tuple-element.14.refs_0_, bf16[256,128]{1,0:T(8,128)(2,1)S(1)} %collective-permute-done.2.refs_1_, bf16[256,128]{1,0:T(8,128)(2,1)S(1)} %collective-permute-done.3.refs_2_, bf16[256,128]{1,0:T(8,128)(2,1)S(1)} %collective-permute-done.4.refs_3_, ...), custom_call_target="tpu_custom_call" | custom-call | flops 1 | bytes 1 | tf_op jit(solution)/shard_map/project/pallas_call | solution.py:274
  (9 shorter events, 0.1 us)
Async XLA Ops:
  0.0 8.9 %copy-start.2 = (f32[16,8]{0,1:T(8,128)S(1)}, f32[16,8]{0,1:T(8,128)}, u32[]{:S(2)}) copy-start(f32[16,8]{0,1:T(8,128)} %param.9) | copy-start | bytes 1540
  0.0 9.0 %collective-permute-start.5 = (bf16[64,2,4096]{2,1,0:T(2,128)(2,1)}, bf16[64,2,4096]{2,1,0:T(2,128)(2,1)S(1)}, u32[]{:S(2)}, u32[]{:S(2)}) collective-permute-start(bf16[64,2,4096]{2,1,0:T(2,128)(2,1)} %param.5), channel_id=1, source_target_pairs={{0,2},{1,3},{2,0},{3,1},{4,6},{5,7},{6,4},{7,5},{8,10},{9,11},{10,... | collective-permute-start | bytes 3145736 | tf_op jit(solution)/shard_map/ppermute | solution.py:192
  1.5 7.5 %collective-permute-start.1 = (s32[2,4,128]{2,1,0:T(4,128)S(1)}, s32[2,4,128]{2,1,0:T(4,128)S(1)}, u32[]{:S(2)}, u32[]{:S(2)}) collective-permute-start(s32[2,4,128]{2,1,0:T(4,128)S(1)} %slice.31), channel_id=1, source_target_pairs={{0,28},{1,29},{2,30},{3,31},{4,0},{5,1},{6,2},{7,3},{8,4},{9,5},{1... | collective-permute-start | bytes 12296 | tf_op jit(solution)/shard_map/ppermute | solution.py:192
  7.2 1.8 %collective-permute-start = (s32[4,128]{1,0:T(4,128)S(1)}, s32[4,128]{1,0:T(4,128)S(1)}, u32[]{:S(2)}, u32[]{:S(2)}) collective-permute-start(s32[4,128]{1,0:T(4,128)S(1)} %get-tuple-element.25), channel_id=1, source_target_pairs={{0,26},{1,27},{2,0},{3,1},{4,30},{5,31},{6,4},{7,5},{8,2},{9,3},{1... | collective-permute-start | bytes 6152 | tf_op jit(solution)/shard_map/ppermute | solution.py:192
  7.4 1.2 %copy-start = (bf16[64,2,4096]{2,1,0:T(2,128)(2,1)S(1)}, bf16[64,2,4096]{2,1,0:T(2,128)(2,1)}, u32[]{:S(2)}) copy-start(bf16[64,2,4096]{2,1,0:T(2,128)(2,1)} %param.5) | copy-start | bytes 3145732
  10.7 8.7 %collective-permute-start.6 = (bf16[256,256]{1,0:T(8,128)(2,1)S(1)}, bf16[256,256]{1,0:T(8,128)(2,1)S(1)}, u32[]{:S(2)}, u32[]{:S(2)}) collective-permute-start(bf16[256,256]{1,0:T(8,128)(2,1)S(1)} %get-tuple-element.19), channel_id=1, source_target_pairs={{0,4},{1,5},{2,6},{3,7},{4,8},{5,9},{6,10},{7,11},{8,12},{9,13},{1... | collective-permute-start | bytes 393224 | tf_op jit(solution)/shard_map/ppermute | solution.py:192
  11.4 11.9 %collective-permute-start.7 = (bf16[256,256]{1,0:T(8,128)(2,1)S(1)}, bf16[256,256]{1,0:T(8,128)(2,1)S(1)}, u32[]{:S(2)}, u32[]{:S(2)}) collective-permute-start(bf16[256,256]{1,0:T(8,128)(2,1)S(1)} %get-tuple-element.20), channel_id=1, source_target_pairs={{0,5},{1,4},{2,7},{3,6},{4,9},{5,8},{6,11},{7,10},{8,13},{9,12},{1... | collective-permute-start | bytes 393224 | tf_op jit(solution)/shard_map/ppermute | solution.py:192
  14.8 2.3 %copy-start.1 = (f32[2,1,2048]{2,1,0:T(1,128)S(1)}, f32[2,1,2048]{2,1,0:T(1,128)}, u32[]{:S(2)}) copy-start(f32[2,1,2048]{2,1,0:T(1,128)} %param.8) | copy-start | bytes 49156
  16.4 7.2 %collective-permute-start.2 = (bf16[256,128]{1,0:T(8,128)(2,1)S(1)}, bf16[256,128]{1,0:T(8,128)(2,1)S(1)}, u32[]{:S(2)}, u32[]{:S(2)}) collective-permute-start(bf16[256,128]{1,0:T(8,128)(2,1)S(1)} %get-tuple-element.15), channel_id=1, source_target_pairs={{0,1},{1,0},{2,3},{3,2},{4,5},{5,4},{6,7},{7,6},{8,9},{9,8},{10,11... | collective-permute-start | bytes 196616 | tf_op jit(solution)/shard_map/ppermute | solution.py:192
  17.1 6.6 %collective-permute-start.3 = (bf16[256,128]{1,0:T(8,128)(2,1)S(1)}, bf16[256,128]{1,0:T(8,128)(2,1)S(1)}, u32[]{:S(2)}, u32[]{:S(2)}) collective-permute-start(bf16[256,128]{1,0:T(8,128)(2,1)S(1)} %get-tuple-element.16), channel_id=1, source_target_pairs={{0,2},{1,3},{2,8},{3,9},{4,6},{5,7},{6,12},{7,13},{8,10},{9,11},{1... | collective-permute-start | bytes 196616 | tf_op jit(solution)/shard_map/ppermute | solution.py:192
  17.1 7.1 %collective-permute-start.4 = (bf16[256,128]{1,0:T(8,128)(2,1)S(1)}, bf16[256,128]{1,0:T(8,128)(2,1)S(1)}, u32[]{:S(2)}, u32[]{:S(2)}) collective-permute-start(bf16[256,128]{1,0:T(8,128)(2,1)S(1)} %get-tuple-element.17), channel_id=1, source_target_pairs={{0,3},{1,2},{2,9},{3,8},{4,7},{5,6},{6,13},{7,12},{8,11},{9,10},{1... | collective-permute-start | bytes 196616 | tf_op jit(solution)/shard_map/ppermute | solution.py:192

commit v5 on v4

--- a/solution.py
+++ b/solution.py
@@ -58,9 +58,9 @@
     tile, group = lax.axis_index("tile"), lax.axis_index("pgroup")
     count = STEPS * groups
     odd = lax.rem(tile, 2)
-    slots = [(0, f) for f in range(groups)]
-    slots += [(3 - 2 * odd, f) for f in range(groups)]
-    slots += [(back, f) for f in range(groups) for back in (2, 1 + 2 * odd)]
+    slots = [(3 - 2 * odd, f) for f in range(groups)]
+    slots += [(0, f) for f in range(groups)]
+    slots += [(back, f) for f in range(groups) for back in (1 + 2 * odd, 2)]
     for s, (back, f) in enumerate(slots):
         block = lax.rem(group + (groups - f), groups) * tiles + lax.rem(tile + (tiles - back), tiles)
         for row in range(2):
@@ -157,18 +157,25 @@
             lax.fori_loop(0, ROW_DEV // 16, fir, 0, unroll=4)
 
 
-def project_kernel(count, first, normaliser, *refs):
+def project_kernel(count, first, *refs):
     pieces, table_ref, out_ref = refs[:count], refs[count], refs[-1]
     left = jnp.concatenate([r[...] for r in pieces], axis=1)
-    rows = table_ref[first : first + left.shape[1], :]
-    image = jnp.dot(left, rows, preferred_element_type=jnp.float32)
-    if len(refs) > count + 2:
-        image = image + refs[count + 1][...]
-    if normaliser is None:
-        out_ref[...] = image
-    else:
-        out_ref[0] = image[:, :COL_DEV] * normaliser
-        out_ref[1] = image[:, COL_DEV:] * normaliser
+    out_ref[...] = jnp.dot(left, table_ref[first : first + left.shape[1], :], preferred_element_type=jnp.float32)
+
+
+def finish_kernel(count, first, normaliser, *refs):
+    pieces, (table_ref, total_ref, out_hbm, made, sems) = refs[:count], refs[count:]
+    left = jnp.concatenate([r[...] for r in pieces], axis=1)
+    rows = pl.ds(first, left.shape[1])
+    copies = []
+    for q in range(2):
+        part = slice(q * COL_DEV, (q + 1) * COL_DEV)
+        image = jnp.dot(left, table_ref[rows, part], preferred_element_type=jnp.float32)
+        made[q] = (image + total_ref[:, part]) * normaliser
+        copies.append(pltpu.make_async_copy(made.at[q], out_hbm.at[q], sems.at[q]))
+        copies[q].start()
+    for copy in copies:
+        copy.wait()
 
 
 def per_device(tiles, groups, echoes, offsets, phase_index, steering, kernels):
@@ -216,17 +223,16 @@
     def block_of(block):
         return lax.dynamic_slice_in_dim(both, block % tiles * pulse_dev, pulse_dev, 1)
 
-    before = tile + tiles - 2
-    blocks = [before, before + 1 - 2 * odd, tile + tiles - 3 + 2 * odd, tile]
+    ahead = tile + tiles
+    blocks = [ahead - 3 + 2 * odd, ahead - 1 - 2 * odd, ahead - 2, tile]
     told = jnp.stack([block_of(block) for block in blocks])
     row = 2 * (told[:, :1] // LANES)
     base = 2 * range_rows * jnp.arange(pulse_dev, dtype=jnp.int32)
     last = jnp.minimum(row + (tall - 4), 2 * range_rows - 8)
     told = jnp.concatenate([base + row, base + last, told[:, :1] % LANES, told[:, 1:]], axis=1)
     told = jnp.concatenate([told, told], axis=2)
-    far_ask = sent(told[2], -3, -1, 0)
-    ask = sent(told[:2], -2, -2, 0)
-    far_ask, ask = lax.optimization_barrier((far_ask, ask))
+    far_ask = sent(told[0], -3, -1, 0)
+    ask = sent(told[1:3], -1, -3, 0)
 
     def profiles(asks, sources, raw, joined):
         count = len(sources)
@@ -251,7 +257,8 @@
         )(*asks, kern, *sources)
 
     near = profiles([ask[0], ask[1]], [mine, theirs], (False, True), True)
-    near = [sent(near[f], 2, 2, f) for f in range(groups)]
+    far_ask, *near = lax.optimization_barrier((far_ask, *near))
+    near = [sent(near[f], 3, 1, f) for f in range(groups)]
     rest = profiles([far_ask, told[3]], [mine, mine], (False, False), False)
     far = [sent(rest[f], 1, 3, f) for f in range(groups)]
     own = [rest[groups]] + [sent(rest[groups + f], 0, 0, f) for f in range(1, groups)]
@@ -268,22 +275,32 @@
         name="steering_table",
     )(steering[:, 0])
 
-    def project(pieces, first, total, last):
-        shape = (2, ROW_DEV, COL_DEV) if last else (ROW_DEV, 2 * COL_DEV)
-        given = list(pieces) + [table] + ([] if total is None else [total])
+    def project(pieces, first):
         return pl.pallas_call(
-            functools.partial(project_kernel, len(pieces), first, normaliser if last else None),
-            out_shape=jax.ShapeDtypeStruct(shape, jnp.float32),
-            in_specs=[whole()] * len(given),
+            functools.partial(project_kernel, len(pieces), first),
+            out_shape=jax.ShapeDtypeStruct((ROW_DEV, 2 * COL_DEV), jnp.float32),
+            in_specs=[whole()] * (len(pieces) + 1),
             out_specs=whole(),
             compiler_params=params,
             cost_estimate=NOTHING,
             name="project",
-        )(*given)
+        )(*pieces, table)
+
+    def finish(pieces, first, total):
+        return pl.pallas_call(
+            functools.partial(finish_kernel, len(pieces), first, normaliser),
+            out_shape=jax.ShapeDtypeStruct((2, ROW_DEV, COL_DEV), jnp.float32),
+            in_specs=[whole()] * (len(pieces) + 2),
+            out_specs=whole(pltpu.HBM),
+            scratch_shapes=[pltpu.VMEM((2, ROW_DEV, COL_DEV), jnp.float32), pltpu.SemaphoreType.DMA((2,))],
+            compiler_params=params,
+            cost_estimate=NOTHING,
+            name="finish",
+        )(*pieces, table, total)
 
     wide = 2 * pulse_dev
-    total = project(near, 2 * groups * wide, None, False)
-    return project(own + far, 0, total, True)
+    total = project(far + own + near[:-1], 0)
+    return finish(near[-1:], (4 * groups - 2) * wide, total)
 
 
 def solution(mesh):

time: 25.4 us -> 24.2 us (0.953)
  waiting for transfers between devices: 5.69 us -> 4.69 us
  starting transfers between devices: 11 us -> 10.7 us
    ppermute x8, waiting for transfers between devices: 5.69 us -> 4.69 us  [sent(): return lax.ppermute(x, ('tile', 'pgroup'), pairs)]
    ppermute x8, starting transfers between devices: 11 us -> 10.7 us  [sent(): return lax.ppermute(x, ('tile', 'pgroup'), pairs)]
  transfers between devices with their start and end apart: 8 -> 8, of which waited for: 3 -> 2; matrix products, arithmetic and copies ran while one was open for 5% -> 5% of each run, Pallas kernels for 13% -> 21%
where the time goes in v5:
time: 24.2 us; the launch traced here: 24 us
  starting transfers between devices  10.7 us (44%)
  Pallas kernels  6.02 us (25%)
  waiting for transfers between devices  4.69 us (19%)
  local copies, waits for them, and re-layouts  1.4 us (6%)
  other arithmetic  1.05 us (4%)
    ppermute x8, starting transfers between devices, sent(): return lax.ppermute(x, ('tile', 'pgroup'), pairs)  10.7 us
    ppermute x8, waiting for transfers between devices, sent(): return lax.ppermute(x, ('tile', 'pgroup'), pairs)  4.69 us
    pallas_call x2, Pallas kernels, profiles(): pl.pallas_call(functools.partial(profile_kernel, pulse_dev, rows, taps, p...  3.36 us
    unnamed x8, local copies, waits for them, and re-layouts  1.31 us
    pallas_call x1, Pallas kernels, per_device(): pl.pallas_call(functools.partial(table_kernel, tiles, groups, pulse_dev),...  1.07 us
    pallas_call x1, Pallas kernels, finish(): pl.pallas_call(functools.partial(finish_kernel, len(pieces), first, norma...  1.04 us
    another operation x2, other arithmetic, per_device(): told = jnp.stack([block_of(block) for block in blocks])  0.85 us
  transfers between devices with their start and end apart: 8, of which 2 were waited for; matrix products, arithmetic and copies ran while one was open for 5% of the time, Pallas kernels for 21%

profile of v5, /device:TPU:0, one launch (start us, length us, event | category | flops | bytes accessed | tf_op | source)
XLA Modules:
  0.0 24.0 jit_solution(9522393581199245620)
XLA Ops:
  0.0 0.0 copy-start.2
  0.0 0.5 %collective-permute-start.2 = (bf16[64,2,4096]{2,1,0:T(2,128)(2,1)}, bf16[64,2,4096]{2,1,0:T(2,128)(2,1)S(1)}, u32[]{:S(2)}, u32[]{:S(2)}) collective-permute-start(bf16[64,2,4096]{2,1,0:T(2,128)(2,1)} %param.5), channel_id=1, source_target_pairs={{0,2},{1,3},{2,0},{3,1},{4,6},{5,7},{6,4},{7,5},{8,10},{9,11},{10,... | collective-permute-start | bytes 3145736 | tf_op jit(solution)/shard_map/ppermute | solution.py:199
  0.5 0.8 %fusion.7 = (s32[1,2,64]{2,1,0:T(2,128)S(1)}, s32[1,2,64]{2,1,0:T(2,128)S(1)}, s32[1,2,64]{2,1,0:T(2,128)S(1)}, s32[1,2,64]{2,1,0:T(2,128)S(1)}) fusion(s32[]{:T(128)S(6)} %select_n.48, s32[1,1024]{1,0:T(1,128)} %param.7, s32[1,1024]{1,0:T(1,128)} %param.6, s32[]{:T(128)S(6)} %select_n.50, s32[]{:T(128)S(6)} %select_n.52, s32[]{:T(128)S(6)} %select_n.54), kind=kLoop, calls=%fused_computation.28 | loop fusion | flops 512 | bytes 10256 | tf_op jit(solution)/shard_map/stack | solution.py:228
  1.4 0.1 add_add_fusion
  1.5 5.7 %collective-permute-start.1 = (s32[2,4,128]{2,1,0:T(4,128)S(1)}, s32[2,4,128]{2,1,0:T(4,128)S(1)}, u32[]{:S(2)}, u32[]{:S(2)}) collective-permute-start(s32[2,4,128]{2,1,0:T(4,128)S(1)} %slice.31), channel_id=1, source_target_pairs={{0,30},{1,31},{2,28},{3,29},{4,2},{5,3},{6,0},{7,1},{8,6},{9,7},{1... | collective-permute-start | bytes 12296 | tf_op jit(solution)/shard_map/ppermute | solution.py:199
  7.2 0.1 add_bitcast_fusion
  7.3 0.1 collective-permute-start
  7.3 0.0 copy-start
  7.3 1.2 %copy-done = bf16[64,2,4096]{2,1,0:T(2,128)(2,1)S(1)} copy-done((bf16[64,2,4096]{2,1,0:T(2,128)(2,1)S(1)}, bf16[64,2,4096]{2,1,0:T(2,128)(2,1)}, u32[]{:S(2)}) %copy-start) | copy-done | bytes 1048600
  8.6 0.2 spread.1.refs_3_.refs_4_
  8.8 0.0 copy-done.2
  8.8 0.1 copy.11
  8.8 0.0 collective-permute-done.1
  8.8 0.0 collective-permute-done.2
  8.9 0.1 broadcast_in_dim.2.refs_2_
  8.9 1.7 %profiles.2 = (bf16[256,256]{1,0:T(8,128)(2,1)S(1)}, bf16[256,256]{1,0:T(8,128)(2,1)S(1)}) custom-call(s32[4,128]{1,0:T(4,128)S(1)} %get-tuple-element.33.refs_0_, s32[4,128]{1,0:T(4,128)S(1)} %get-tuple-element.32.refs_1_, f32[16,8,128]{2,1,0:T(8,128)S(1)} %broadcast_in_dim.2.refs_2_, f32[4096,128]{1,0:T(8,128)S(1)} %spread.1.refs_3_.refs_4_, ...), custom_call_target="tpu_custom_call" | custom-call | flops 1 | bytes 1 | tf_op jit(solution)/shard_map/profiles/pallas_call | solution.py:241
  10.6 0.0 collective-permute-done.refs_0_
  10.6 0.1 collective-permute-start.7
  10.7 3.7 %collective-permute-start.3 = (bf16[256,256]{1,0:T(8,128)(2,1)S(1)}, bf16[256,256]{1,0:T(8,128)(2,1)S(1)}, u32[]{:S(2)}, u32[]{:S(2)}) collective-permute-start(bf16[256,256]{1,0:T(8,128)(2,1)S(1)} %get-tuple-element.16), channel_id=1, source_target_pairs={{0,7},{1,6},{2,5},{3,4},{4,11},{5,10},{6,9},{7,8},{8,15},{9,14},{1... | collective-permute-start | bytes 393224 | tf_op jit(solution)/shard_map/ppermute | solution.py:199
  14.4 1.7 %profiles.3 = (bf16[256,128]{1,0:T(8,128)(2,1)S(1)}, bf16[256,128]{1,0:T(8,128)(2,1)S(1)}, bf16[256,128]{1,0:T(8,128)(2,1)S(1)}, bf16[256,128]{1,0:T(8,128)(2,1)S(1)}) custom-call(s32[4,128]{1,0:T(4,128)S(1)} %collective-permute-done.refs_0_, s32[4,128]{1,0:T(4,128)S(1)} %get-tuple-element.26.refs_1_, f32[16,8,128]{2,1,0:T(8,128)S(1)} %broadcast_in_dim.2.refs_2_, ...), custom_call_target="tpu_custom_call" | custom-call | flops 1 | bytes 1 | tf_op jit(solution)/shard_map/profiles/pallas_call | solution.py:241
  16.1 0.1 collective-permute-start.4
  16.1 0.1 collective-permute-start.5
  16.2 0.6 %collective-permute-start.6 = (bf16[256,128]{1,0:T(8,128)(2,1)S(1)}, bf16[256,128]{1,0:T(8,128)(2,1)S(1)}, u32[]{:S(2)}, u32[]{:S(2)}) collective-permute-start(bf16[256,128]{1,0:T(8,128)(2,1)S(1)} %get-tuple-element.21), channel_id=1, source_target_pairs={{0,1},{1,0},{2,3},{3,2},{4,5},{5,4},{6,7},{7,6},{8,9},{9,8},{10,11... | collective-permute-start | bytes 196616 | tf_op jit(solution)/shard_map/ppermute | solution.py:199
  16.8 0.0 copy-done.1
  16.8 1.1 %steering_table.1.refs_5_.refs_1_ = bf16[1024,512]{1,0:T(8,128)(2,1)S(1)} custom-call(f32[2,2048]{1,0:T(2,128)S(1)} %bitcast.32), custom_call_target="tpu_custom_call" | custom-call | flops 1 | bytes 1 | tf_op jit(solution)/shard_map/steering_table/pallas_call | solution.py:267
  17.9 3.7 %collective-permute-done.4.refs_0_ = bf16[256,128]{1,0:T(8,128)(2,1)S(1)} collective-permute-done((bf16[256,128]{1,0:T(8,128)(2,1)S(1)}, bf16[256,128]{1,0:T(8,128)(2,1)S(1)}, u32[]{:S(2)}, u32[]{:S(2)}) %collective-permute-start.4) | collective-permute-done | bytes 65568 | tf_op jit(solution)/shard_map/ppermute | solution.py:199
  21.6 1.0 %collective-permute-done.5.refs_1_ = bf16[256,128]{1,0:T(8,128)(2,1)S(1)} collective-permute-done((bf16[256,128]{1,0:T(8,128)(2,1)S(1)}, bf16[256,128]{1,0:T(8,128)(2,1)S(1)}, u32[]{:S(2)}, u32[]{:S(2)}) %collective-permute-start.5) | collective-permute-done | bytes 65568 | tf_op jit(solution)/shard_map/ppermute | solution.py:199
  22.6 0.0 collective-permute-done.6.refs_3_
  22.6 0.0 collective-permute-done.7.refs_4_
  22.6 0.4 %project.1.refs_2_ = f32[256,512]{1,0:T(8,128)S(1)} custom-call(bf16[256,128]{1,0:T(8,128)(2,1)S(1)} %collective-permute-done.4.refs_0_, bf16[256,128]{1,0:T(8,128)(2,1)S(1)} %collective-permute-done.5.refs_1_, bf16[256,128]{1,0:T(8,128)(2,1)S(1)} %get-tuple-element.20.refs_2_, bf16[256,128]{1,0:T(8,128)(2,1)S(1)} %collective-permute-done.6.refs_3_, ...), custom_call_target="tpu_custom_call" | custom-call | flops 1 | bytes 1 | tf_op jit(solution)/shard_map/project/pallas_call | solution.py:279
  22.9 0.0 collective-permute-done.3.refs_0_
  22.9 1.0 %finish.1 = f32[2,256,256]{2,1,0:T(8,128)} custom-call(bf16[256,256]{1,0:T(8,128)(2,1)S(1)} %collective-permute-done.3.refs_0_, bf16[1024,512]{1,0:T(8,128)(2,1)S(1)} %steering_table.1.refs_5_.refs_1_, f32[256,512]{1,0:T(8,128)S(1)} %project.1.refs_2_), custom_call_target="tpu_custom_call" | custom-call | flops 1 | bytes 1 | tf_op jit(solution)/shard_map/finish/pallas_call | solution.py:290
  (9 shorter events, 0.1 us)
Async XLA Ops:
  0.0 8.8 %copy-start.2 = (f32[16,8]{0,1:T(8,128)S(1)}, f32[16,8]{0,1:T(8,128)}, u32[]{:S(2)}) copy-start(f32[16,8]{0,1:T(8,128)} %param.9) | copy-start | bytes 1540
  0.0 8.8 %collective-permute-start.2 = (bf16[64,2,4096]{2,1,0:T(2,128)(2,1)}, bf16[64,2,4096]{2,1,0:T(2,128)(2,1)S(1)}, u32[]{:S(2)}, u32[]{:S(2)}) collective-permute-start(bf16[64,2,4096]{2,1,0:T(2,128)(2,1)} %param.5), channel_id=1, source_target_pairs={{0,2},{1,3},{2,0},{3,1},{4,6},{5,7},{6,4},{7,5},{8,10},{9,11},{10,... | collective-permute-start | bytes 3145736 | tf_op jit(solution)/shard_map/ppermute | solution.py:199
  1.5 7.4 %collective-permute-start.1 = (s32[2,4,128]{2,1,0:T(4,128)S(1)}, s32[2,4,128]{2,1,0:T(4,128)S(1)}, u32[]{:S(2)}, u32[]{:S(2)}) collective-permute-start(s32[2,4,128]{2,1,0:T(4,128)S(1)} %slice.31), channel_id=1, source_target_pairs={{0,30},{1,31},{2,28},{3,29},{4,2},{5,3},{6,0},{7,1},{8,6},{9,7},{1... | collective-permute-start | bytes 12296 | tf_op jit(solution)/shard_map/ppermute | solution.py:199
  7.3 3.4 %collective-permute-start = (s32[4,128]{1,0:T(4,128)S(1)}, s32[4,128]{1,0:T(4,128)S(1)}, u32[]{:S(2)}, u32[]{:S(2)}) collective-permute-start(s32[4,128]{1,0:T(4,128)S(1)} %get-tuple-element.27), channel_id=1, source_target_pairs={{0,26},{1,27},{2,0},{3,1},{4,30},{5,31},{6,4},{7,5},{8,2},{9,3},{1... | collective-permute-start | bytes 6152 | tf_op jit(solution)/shard_map/ppermute | solution.py:199
  7.3 1.2 %copy-start = (bf16[64,2,4096]{2,1,0:T(2,128)(2,1)S(1)}, bf16[64,2,4096]{2,1,0:T(2,128)(2,1)}, u32[]{:S(2)}) copy-start(bf16[64,2,4096]{2,1,0:T(2,128)(2,1)} %param.5) | copy-start | bytes 3145732
  10.6 11.9 %collective-permute-start.7 = (bf16[256,256]{1,0:T(8,128)(2,1)S(1)}, bf16[256,256]{1,0:T(8,128)(2,1)S(1)}, u32[]{:S(2)}, u32[]{:S(2)}) collective-permute-start(bf16[256,256]{1,0:T(8,128)(2,1)S(1)} %get-tuple-element.22), channel_id=1, source_target_pairs={{0,6},{1,7},{2,4},{3,5},{4,10},{5,11},{6,8},{7,9},{8,14},{9,15},{1... | collective-permute-start | bytes 393224 | tf_op jit(solution)/shard_map/ppermute | solution.py:199
  10.7 12.2 %collective-permute-start.3 = (bf16[256,256]{1,0:T(8,128)(2,1)S(1)}, bf16[256,256]{1,0:T(8,128)(2,1)S(1)}, u32[]{:S(2)}, u32[]{:S(2)}) collective-permute-start(bf16[256,256]{1,0:T(8,128)(2,1)S(1)} %get-tuple-element.16), channel_id=1, source_target_pairs={{0,7},{1,6},{2,5},{3,4},{4,11},{5,10},{6,9},{7,8},{8,15},{9,14},{1... | collective-permute-start | bytes 393224 | tf_op jit(solution)/shard_map/ppermute | solution.py:199
  14.4 2.4 %copy-start.1 = (f32[2,1,2048]{2,1,0:T(1,128)S(1)}, f32[2,1,2048]{2,1,0:T(1,128)}, u32[]{:S(2)}) copy-start(f32[2,1,2048]{2,1,0:T(1,128)} %param.8) | copy-start | bytes 49156
  16.1 5.5 %collective-permute-start.4 = (bf16[256,128]{1,0:T(8,128)(2,1)S(1)}, bf16[256,128]{1,0:T(8,128)(2,1)S(1)}, u32[]{:S(2)}, u32[]{:S(2)}) collective-permute-start(bf16[256,128]{1,0:T(8,128)(2,1)S(1)} %get-tuple-element.18), channel_id=1, source_target_pairs={{0,2},{1,3},{2,8},{3,9},{4,6},{5,7},{6,12},{7,13},{8,10},{9,11},{1... | collective-permute-start | bytes 196616 | tf_op jit(solution)/shard_map/ppermute | solution.py:199
  16.1 6.4 %collective-permute-start.5 = (bf16[256,128]{1,0:T(8,128)(2,1)S(1)}, bf16[256,128]{1,0:T(8,128)(2,1)S(1)}, u32[]{:S(2)}, u32[]{:S(2)}) collective-permute-start(bf16[256,128]{1,0:T(8,128)(2,1)S(1)} %get-tuple-element.19), channel_id=1, source_target_pairs={{0,3},{1,2},{2,9},{3,8},{4,7},{5,6},{6,13},{7,12},{8,11},{9,10},{1... | collective-permute-start | bytes 196616 | tf_op jit(solution)/shard_map/ppermute | solution.py:199
  16.2 6.4 %collective-permute-start.6 = (bf16[256,128]{1,0:T(8,128)(2,1)S(1)}, bf16[256,128]{1,0:T(8,128)(2,1)S(1)}, u32[]{:S(2)}, u32[]{:S(2)}) collective-permute-start(bf16[256,128]{1,0:T(8,128)(2,1)S(1)} %get-tuple-element.21), channel_id=1, source_target_pairs={{0,1},{1,0},{2,3},{3,2},{4,5},{5,4},{6,7},{7,6},{8,9},{9,8},{10,11... | collective-permute-start | bytes 196616 | tf_op jit(solution)/shard_map/ppermute | solution.py:199

commit v6 on v5

--- a/solution.py
+++ b/solution.py
@@ -40,6 +40,10 @@
     return pl.BlockSpec(memory_space=space)
 
 
+def send_order(groups):
+    return list(range(groups))[::-1]
+
+
 def block_twice(ref, row, block, width):
     per = LANES // width
     at = pl.multiple_of(block // per * LANES, LANES)
@@ -58,9 +62,11 @@
     tile, group = lax.axis_index("tile"), lax.axis_index("pgroup")
     count = STEPS * groups
     odd = lax.rem(tile, 2)
-    slots = [(3 - 2 * odd, f) for f in range(groups)]
+    order = send_order(groups)
+    slots = [(3 - 2 * odd, f) for f in order]
+    slots += [(back, f) for f in order[:-1] for back in (1 + 2 * odd, 2)]
     slots += [(0, f) for f in range(groups)]
-    slots += [(back, f) for f in range(groups) for back in (1 + 2 * odd, 2)]
+    slots += [(back, order[-1]) for back in (1 + 2 * odd, 2)]
     for s, (back, f) in enumerate(slots):
         block = lax.rem(group + (groups - f), groups) * tiles + lax.rem(tile + (tiles - back), tiles)
         for row in range(2):
@@ -104,7 +110,7 @@
     count = len(raw)
     asks, kern_ref, refs = refs[:count], refs[count], refs[count + 1 :]
     echoes, refs = list(refs[:count]), refs[count:]
-    outs, (wide, tail, turned, scalars, sems, *spare) = refs[: groups * (1 if joined else count)], refs[-5 - sum(raw) :]
+    outs, (wide, tail, turned, scalars, sems, *spare) = refs[: groups * (1 if joined else count)], refs[-5 - raw.count(True) :]
     copies = [pltpu.make_async_copy(asks[i], scalars.at[i], sems.at[i]) for i in range(count)]
     for copy in copies:
         copy.start()
@@ -120,6 +126,7 @@
         kerns.append(kern)
         if raw[i]:
             spread_rows(echoes[i], spare[0])
+        if raw[i] is not False:
             echoes[i] = spare[0]
 
     for i in range(count):
@@ -214,8 +221,8 @@
         )(in_pairs(x))
 
     partner = sent(echoes, 1, -1, 0)
-    mine = spread(echoes)
-    theirs = in_pairs(partner)
+    theirs = spread(partner)
+    held, theirs = lax.optimization_barrier((echoes, theirs))
     kern = jnp.broadcast_to(kernels[:, :, None], (phases, taps, 2 * pulse_dev))
 
     both = jnp.concatenate([offsets, phase_index], axis=0)
@@ -250,16 +257,16 @@
                 pltpu.SMEM((count, 4, 2 * pulse_dev), jnp.int32),
                 pltpu.SemaphoreType.DMA((count,)),
             ]
-            + [pltpu.VMEM((pulse_dev * 2 * range_rows, LANES), jnp.float32)] * sum(raw),
+            + [pltpu.VMEM((pulse_dev * 2 * range_rows, LANES), jnp.float32)] * raw.count(True),
             compiler_params=params,
             cost_estimate=NOTHING,
             name="profiles",
         )(*asks, kern, *sources)
 
-    near = profiles([ask[0], ask[1]], [mine, theirs], (False, True), True)
+    near = profiles([ask[0], ask[1]], [in_pairs(held), theirs], (True, False), True)
     far_ask, *near = lax.optimization_barrier((far_ask, *near))
     near = [sent(near[f], 3, 1, f) for f in range(groups)]
-    rest = profiles([far_ask, told[3]], [mine, mine], (False, False), False)
+    rest = profiles([far_ask, told[3]], [in_pairs(held)] * 2, (True, None), False)
     far = [sent(rest[f], 1, 3, f) for f in range(groups)]
     own = [rest[groups]] + [sent(rest[groups + f], 0, 0, f) for f in range(1, groups)]
 
@@ -299,8 +306,9 @@
         )(*pieces, table, total)
 
     wide = 2 * pulse_dev
-    total = project(far + own + near[:-1], 0)
-    return finish(near[-1:], (4 * groups - 2) * wide, total)
+    order = send_order(groups)
+    total = project([far[f] for f in order] + [near[f] for f in order[:-1]], 0)
+    return finish(own + [near[order[-1]]], (3 * groups - 2) * wide, total)
 
 
 def solution(mesh):

time: 24.2 us -> 24 us (level)
  waiting for transfers between devices: 4.69 us -> 5.29 us
  local copies, waits for them, and re-layouts: 1.4 us -> 0.86 us
  starting transfers between devices: 10.7 us -> 10.4 us
    ppermute x8, waiting for transfers between devices: 4.69 us -> 5.29 us  [sent(): return lax.ppermute(x, ('tile', 'pgroup'), pairs)]
    unnamed x8 -> x6, local copies, waits for them, and re-layouts: 1.31 us -> 0.78 us
    ppermute x8, starting transfers between devices: 10.7 us -> 10.4 us  [sent(): return lax.ppermute(x, ('tile', 'pgroup'), pairs)]
  transfers between devices with their start and end apart: 8 -> 8, of which waited for: 2 -> 3; matrix products, arithmetic and copies ran while one was open for 5% -> 8% of each run, Pallas kernels for 21% -> 21%
where the time goes in v6:
time: 24 us; the launch traced here: 23.8 us
  starting transfers between devices  10.4 us (43%)
  Pallas kernels  6.02 us (25%)
  waiting for transfers between devices  5.29 us (22%)
  other arithmetic  1.05 us (4%)
  local copies, waits for them, and re-layouts  0.86 us (4%)
    ppermute x8, starting transfers between devices, sent(): return lax.ppermute(x, ('tile', 'pgroup'), pairs)  10.4 us
    ppermute x8, waiting for transfers between devices, sent(): return lax.ppermute(x, ('tile', 'pgroup'), pairs)  5.29 us
    pallas_call x2, Pallas kernels, profiles(): pl.pallas_call(functools.partial(profile_kernel, pulse_dev, rows, taps, p...  3.35 us
    pallas_call x1, Pallas kernels, finish(): pl.pallas_call(functools.partial(finish_kernel, len(pieces), first, norma...  1.11 us
    pallas_call x1, Pallas kernels, per_device(): pl.pallas_call(functools.partial(table_kernel, tiles, groups, pulse_dev),...  1.07 us
    another operation x2, other arithmetic, per_device(): told = jnp.stack([block_of(block) for block in blocks])  0.85 us
    unnamed x6, local copies, waits for them, and re-layouts  0.78 us
  transfers between devices with their start and end apart: 8, of which 3 were waited for; matrix products, arithmetic and copies ran while one was open for 8% of the time, Pallas kernels for 21%

profile of v6, /device:TPU:0, one launch (start us, length us, event | category | flops | bytes accessed | tf_op | source)
XLA Modules:
  0.0 23.8 jit_solution(18173438165501181227)
XLA Ops:
  0.0 0.0 copy-start
  0.0 0.5 %collective-permute-start.2 = (bf16[64,2,4096]{2,1,0:T(2,128)(2,1)}, bf16[64,2,4096]{2,1,0:T(2,128)(2,1)S(1)}, u32[]{:S(2)}, u32[]{:S(2)}) collective-permute-start(bf16[64,2,4096]{2,1,0:T(2,128)(2,1)} %param.5), channel_id=1, source_target_pairs={{0,2},{1,3},{2,0},{3,1},{4,6},{5,7},{6,4},{7,5},{8,10},{9,11},{10,... | collective-permute-start | bytes 3145736 | tf_op jit(solution)/shard_map/ppermute | solution.py:206
  0.5 0.8 %fusion.7 = (s32[1,2,64]{2,1,0:T(2,128)S(1)}, s32[1,2,64]{2,1,0:T(2,128)S(1)}, s32[1,2,64]{2,1,0:T(2,128)S(1)}, s32[1,2,64]{2,1,0:T(2,128)S(1)}) fusion(s32[]{:T(128)S(6)} %select_n.48, s32[1,1024]{1,0:T(1,128)} %param.7, s32[1,1024]{1,0:T(1,128)} %param.6, s32[]{:T(128)S(6)} %select_n.50, s32[]{:T(128)S(6)} %select_n.52, s32[]{:T(128)S(6)} %select_n.54), kind=kLoop, calls=%fused_computation.28 | loop fusion | flops 512 | bytes 10256 | tf_op jit(solution)/shard_map/stack | solution.py:235
  1.4 0.1 add_add_fusion
  1.5 5.7 %collective-permute-start.1 = (s32[2,4,128]{2,1,0:T(4,128)S(1)}, s32[2,4,128]{2,1,0:T(4,128)S(1)}, u32[]{:S(2)}, u32[]{:S(2)}) collective-permute-start(s32[2,4,128]{2,1,0:T(4,128)S(1)} %slice.31), channel_id=1, source_target_pairs={{0,30},{1,31},{2,28},{3,29},{4,2},{5,3},{6,0},{7,1},{8,6},{9,7},{1... | collective-permute-start | bytes 12296 | tf_op jit(solution)/shard_map/ppermute | solution.py:206
  7.2 0.1 add_bitcast_fusion
  7.3 0.1 collective-permute-start
  7.4 0.8 %copy.11 = f32[16,8]{1,0:T(8,128)S(1)} copy(f32[16,8]{0,1:T(8,128)} %param.9) | data formatting | bytes 1024 | tf_op args[4]
  8.2 0.4 %collective-permute-done.1 = s32[2,4,128]{2,1,0:T(4,128)S(1)} collective-permute-done((s32[2,4,128]{2,1,0:T(4,128)S(1)}, s32[2,4,128]{2,1,0:T(4,128)S(1)}, u32[]{:S(2)}, u32[]{:S(2)}) %collective-permute-start.1) | collective-permute-done | bytes 4128 | tf_op jit(solution)/shard_map/ppermute | solution.py:206
  8.5 0.0 collective-permute-done.2
  8.5 0.2 spread.1.refs_4_
  8.7 0.1 broadcast_in_dim.2.refs_2_
  8.8 0.0 copy-done
  8.8 0.0 copy-start.1
  8.8 1.7 %profiles.2 = (bf16[256,256]{1,0:T(8,128)(2,1)S(1)}, bf16[256,256]{1,0:T(8,128)(2,1)S(1)}) custom-call(s32[4,128]{1,0:T(4,128)S(1)} %get-tuple-element.37.refs_0_, s32[4,128]{1,0:T(4,128)S(1)} %get-tuple-element.36.refs_1_, f32[16,8,128]{2,1,0:T(8,128)S(1)} %broadcast_in_dim.2.refs_2_, bf16[4096,128]{1,0:T(8,128)(2,1)S(1)} %bitcast.30, ...), custom_call_target="tpu_custom_call" | custom-call | flops 1 | bytes 1 | tf_op jit(solution)/shard_map/profiles/pallas_call | solution.py:248
  10.5 0.0 collective-permute-done.refs_0_
  10.5 0.5 %collective-permute-start.7 = (bf16[256,256]{1,0:T(8,128)(2,1)S(1)}, bf16[256,256]{1,0:T(8,128)(2,1)S(1)}, u32[]{:S(2)}, u32[]{:S(2)}) collective-permute-start(bf16[256,256]{1,0:T(8,128)(2,1)S(1)} %get-tuple-element.26), channel_id=1, source_target_pairs={{0,7},{1,6},{2,5},{3,4},{4,11},{5,10},{6,9},{7,8},{8,15},{9,14},{1... | collective-permute-start | bytes 393224 | tf_op jit(solution)/shard_map/ppermute | solution.py:206
  11.1 2.9 %collective-permute-start.4 = (bf16[256,256]{1,0:T(8,128)(2,1)S(1)}, bf16[256,256]{1,0:T(8,128)(2,1)S(1)}, u32[]{:S(2)}, u32[]{:S(2)}) collective-permute-start(bf16[256,256]{1,0:T(8,128)(2,1)S(1)} %get-tuple-element.23), channel_id=1, source_target_pairs={{0,6},{1,7},{2,4},{3,5},{4,10},{5,11},{6,8},{7,9},{8,14},{9,15},{1... | collective-permute-start | bytes 393224 | tf_op jit(solution)/shard_map/ppermute | solution.py:206
  13.9 1.7 %profiles.3 = (bf16[256,128]{1,0:T(8,128)(2,1)S(1)}, bf16[256,128]{1,0:T(8,128)(2,1)S(1)}, bf16[256,128]{1,0:T(8,128)(2,1)S(1)}, bf16[256,128]{1,0:T(8,128)(2,1)S(1)}) custom-call(s32[4,128]{1,0:T(4,128)S(1)} %collective-permute-done.refs_0_, s32[4,128]{1,0:T(4,128)S(1)} %get-tuple-element.30.refs_1_, f32[16,8,128]{2,1,0:T(8,128)S(1)} %broadcast_in_dim.2.refs_2_, ...), custom_call_target="tpu_custom_call" | custom-call | flops 1 | bytes 1 | tf_op jit(solution)/shard_map/profiles/pallas_call | solution.py:248
  15.6 0.1 collective-permute-start.5
  15.7 0.1 collective-permute-start.6
  15.7 0.6 %collective-permute-start.3 = (bf16[256,128]{1,0:T(8,128)(2,1)S(1)}, bf16[256,128]{1,0:T(8,128)(2,1)S(1)}, u32[]{:S(2)}, u32[]{:S(2)}) collective-permute-start(bf16[256,128]{1,0:T(8,128)(2,1)S(1)} %get-tuple-element.22), channel_id=1, source_target_pairs={{0,1},{1,0},{2,3},{3,2},{4,5},{5,4},{6,7},{7,6},{8,9},{9,8},{10,11... | collective-permute-start | bytes 196616 | tf_op jit(solution)/shard_map/ppermute | solution.py:206
  16.3 0.0 copy-done.1
  16.4 1.1 %steering_table.1.refs_3_ = bf16[1024,512]{1,0:T(8,128)(2,1)S(1)} custom-call(f32[2,2048]{1,0:T(2,128)S(1)} %bitcast.34), custom_call_target="tpu_custom_call" | custom-call | flops 1 | bytes 1 | tf_op jit(solution)/shard_map/steering_table/pallas_call | solution.py:274
  17.4 4.6 %collective-permute-done.5.refs_0_ = bf16[256,128]{1,0:T(8,128)(2,1)S(1)} collective-permute-done((bf16[256,128]{1,0:T(8,128)(2,1)S(1)}, bf16[256,128]{1,0:T(8,128)(2,1)S(1)}, u32[]{:S(2)}, u32[]{:S(2)}) %collective-permute-start.5) | collective-permute-done | bytes 65568 | tf_op jit(solution)/shard_map/ppermute | solution.py:206
  22.1 0.0 collective-permute-done.6.refs_1_
  22.1 0.0 collective-permute-done.7.refs_2_
  22.1 0.3 %project.1.refs_4_ = f32[256,512]{1,0:T(8,128)S(1)} custom-call(bf16[256,128]{1,0:T(8,128)(2,1)S(1)} %collective-permute-done.5.refs_0_, bf16[256,128]{1,0:T(8,128)(2,1)S(1)} %collective-permute-done.6.refs_1_, bf16[256,256]{1,0:T(8,128)(2,1)S(1)} %collective-permute-done.7.refs_2_, bf16[1024,512]{1,0:T(8,128)(2,1)S(1)} %steering_table.1.refs_3_), custom_call_target="tpu_custom_call" | custom-call | flops 1 | bytes 1 | tf_op jit(solution)/shard_map/project/pallas_call | solution.py:286
  22.4 0.0 collective-permute-done.3.refs_1_
  22.4 0.3 %collective-permute-done.4.refs_2_ = bf16[256,256]{1,0:T(8,128)(2,1)S(1)} collective-permute-done((bf16[256,256]{1,0:T(8,128)(2,1)S(1)}, bf16[256,256]{1,0:T(8,128)(2,1)S(1)}, u32[]{:S(2)}, u32[]{:S(2)}) %collective-permute-start.4) | collective-permute-done | bytes 131104 | tf_op jit(solution)/shard_map/ppermute | solution.py:206
  22.7 1.1 %finish.1 = f32[2,256,256]{2,1,0:T(8,128)} custom-call(bf16[256,128]{1,0:T(8,128)(2,1)S(1)} %get-tuple-element.21.refs_0_, bf16[256,128]{1,0:T(8,128)(2,1)S(1)} %collective-permute-done.3.refs_1_, bf16[256,256]{1,0:T(8,128)(2,1)S(1)} %collective-permute-done.4.refs_2_, bf16[1024,512]{1,0:T(8,128)(2,1)S(1)} %steering_table.1.refs_3_, ...), custom_call_target="tpu_custom_call" | custom-call | flops 1 | bytes 1 | tf_op jit(solution)/shard_map/finish/pallas_call | solution.py:297
  (8 shorter events, 0.1 us)
Async XLA Ops:
  0.0 8.8 %copy-start = (bf16[64,2,4096]{2,1,0:T(2,128)(2,1)S(1)}, bf16[64,2,4096]{2,1,0:T(2,128)(2,1)}, u32[]{:S(2)}) copy-start(bf16[64,2,4096]{2,1,0:T(2,128)(2,1)} %param.5) | copy-start | bytes 3145732
  0.0 8.5 %collective-permute-start.2 = (bf16[64,2,4096]{2,1,0:T(2,128)(2,1)}, bf16[64,2,4096]{2,1,0:T(2,128)(2,1)S(1)}, u32[]{:S(2)}, u32[]{:S(2)}) collective-permute-start(bf16[64,2,4096]{2,1,0:T(2,128)(2,1)} %param.5), channel_id=1, source_target_pairs={{0,2},{1,3},{2,0},{3,1},{4,6},{5,7},{6,4},{7,5},{8,10},{9,11},{10,... | collective-permute-start | bytes 3145736 | tf_op jit(solution)/shard_map/ppermute | solution.py:206
  1.5 7.1 %collective-permute-start.1 = (s32[2,4,128]{2,1,0:T(4,128)S(1)}, s32[2,4,128]{2,1,0:T(4,128)S(1)}, u32[]{:S(2)}, u32[]{:S(2)}) collective-permute-start(s32[2,4,128]{2,1,0:T(4,128)S(1)} %slice.31), channel_id=1, source_target_pairs={{0,30},{1,31},{2,28},{3,29},{4,2},{5,3},{6,0},{7,1},{8,6},{9,7},{1... | collective-permute-start | bytes 12296 | tf_op jit(solution)/shard_map/ppermute | solution.py:206
  7.3 3.2 %collective-permute-start = (s32[4,128]{1,0:T(4,128)S(1)}, s32[4,128]{1,0:T(4,128)S(1)}, u32[]{:S(2)}, u32[]{:S(2)}) collective-permute-start(s32[4,128]{1,0:T(4,128)S(1)} %get-tuple-element.31), channel_id=1, source_target_pairs={{0,26},{1,27},{2,0},{3,1},{4,30},{5,31},{6,4},{7,5},{8,2},{9,3},{1... | collective-permute-start | bytes 6152 | tf_op jit(solution)/shard_map/ppermute | solution.py:206
  8.8 7.5 %copy-start.1 = (f32[2,1,2048]{2,1,0:T(1,128)S(1)}, f32[2,1,2048]{2,1,0:T(1,128)}, u32[]{:S(2)}) copy-start(f32[2,1,2048]{2,1,0:T(1,128)} %param.8) | copy-start | bytes 49156
  10.5 11.5 %collective-permute-start.7 = (bf16[256,256]{1,0:T(8,128)(2,1)S(1)}, bf16[256,256]{1,0:T(8,128)(2,1)S(1)}, u32[]{:S(2)}, u32[]{:S(2)}) collective-permute-start(bf16[256,256]{1,0:T(8,128)(2,1)S(1)} %get-tuple-element.26), channel_id=1, source_target_pairs={{0,7},{1,6},{2,5},{3,4},{4,11},{5,10},{6,9},{7,8},{8,15},{9,14},{1... | collective-permute-start | bytes 393224 | tf_op jit(solution)/shard_map/ppermute | solution.py:206
  11.1 11.6 %collective-permute-start.4 = (bf16[256,256]{1,0:T(8,128)(2,1)S(1)}, bf16[256,256]{1,0:T(8,128)(2,1)S(1)}, u32[]{:S(2)}, u32[]{:S(2)}) collective-permute-start(bf16[256,256]{1,0:T(8,128)(2,1)S(1)} %get-tuple-element.23), channel_id=1, source_target_pairs={{0,6},{1,7},{2,4},{3,5},{4,10},{5,11},{6,8},{7,9},{8,14},{9,15},{1... | collective-permute-start | bytes 393224 | tf_op jit(solution)/shard_map/ppermute | solution.py:206
  15.6 6.4 %collective-permute-start.5 = (bf16[256,128]{1,0:T(8,128)(2,1)S(1)}, bf16[256,128]{1,0:T(8,128)(2,1)S(1)}, u32[]{:S(2)}, u32[]{:S(2)}) collective-permute-start(bf16[256,128]{1,0:T(8,128)(2,1)S(1)} %get-tuple-element.24), channel_id=1, source_target_pairs={{0,3},{1,2},{2,9},{3,8},{4,7},{5,6},{6,13},{7,12},{8,11},{9,10},{1... | collective-permute-start | bytes 196616 | tf_op jit(solution)/shard_map/ppermute | solution.py:206
  15.7 6.4 %collective-permute-start.6 = (bf16[256,128]{1,0:T(8,128)(2,1)S(1)}, bf16[256,128]{1,0:T(8,128)(2,1)S(1)}, u32[]{:S(2)}, u32[]{:S(2)}) collective-permute-start(bf16[256,128]{1,0:T(8,128)(2,1)S(1)} %get-tuple-element.25), channel_id=1, source_target_pairs={{0,2},{1,3},{2,8},{3,9},{4,6},{5,7},{6,12},{7,13},{8,10},{9,11},{1... | collective-permute-start | bytes 196616 | tf_op jit(solution)/shard_map/ppermute | solution.py:206
  15.7 6.6 %collective-permute-start.3 = (bf16[256,128]{1,0:T(8,128)(2,1)S(1)}, bf16[256,128]{1,0:T(8,128)(2,1)S(1)}, u32[]{:S(2)}, u32[]{:S(2)}) collective-permute-start(bf16[256,128]{1,0:T(8,128)(2,1)S(1)} %get-tuple-element.22), channel_id=1, source_target_pairs={{0,1},{1,0},{2,3},{3,2},{4,5},{5,4},{6,7},{7,6},{8,9},{9,8},{10,11... | collective-permute-start | bytes 196616 | tf_op jit(solution)/shard_map/ppermute | solution.py:206

commit v7 on v6

--- a/solution.py
+++ b/solution.py
@@ -263,6 +263,7 @@
             name="profiles",
         )(*asks, kern, *sources)
 
+    theirs, ask = lax.optimization_barrier((theirs, ask))
     near = profiles([ask[0], ask[1]], [in_pairs(held), theirs], (True, False), True)
     far_ask, *near = lax.optimization_barrier((far_ask, *near))
     near = [sent(near[f], 3, 1, f) for f in range(groups)]

time: 24 us -> 23.7 us (0.987)
  waiting for transfers between devices: 5.29 us -> 4.78 us
  starting transfers between devices: 10.4 us -> 10.7 us
    ppermute x8, waiting for transfers between devices: 5.29 us -> 4.78 us  [sent(): return lax.ppermute(x, ('tile', 'pgroup'), pairs)]
  transfers between devices with their start and end apart: 8 -> 8, of which waited for: 3 -> 2; matrix products, arithmetic and copies ran while one was open for 8% -> 8% of each run, Pallas kernels for 21% -> 21%
where the time goes in v7:
time: 23.7 us; the launch traced here: 23.5 us
  starting transfers between devices  10.7 us (45%)
  Pallas kernels  6.02 us (25%)
  waiting for transfers between devices  4.78 us (20%)
  other arithmetic  1.05 us (4%)
  local copies, waits for them, and re-layouts  0.86 us (4%)
    ppermute x8, starting transfers between devices, sent(): return lax.ppermute(x, ('tile', 'pgroup'), pairs)  10.7 us
    ppermute x8, waiting for transfers between devices, sent(): return lax.ppermute(x, ('tile', 'pgroup'), pairs)  4.78 us
    pallas_call x2, Pallas kernels, profiles(): pl.pallas_call(functools.partial(profile_kernel, pulse_dev, rows, taps, p...  3.35 us
    pallas_call x1, Pallas kernels, finish(): pl.pallas_call(functools.partial(finish_kernel, len(pieces), first, norma...  1.11 us
    pallas_call x1, Pallas kernels, per_device(): pl.pallas_call(functools.partial(table_kernel, tiles, groups, pulse_dev),...  1.07 us
    another operation x2, other arithmetic, per_device(): told = jnp.stack([block_of(block) for block in blocks])  0.85 us
    unnamed x6, local copies, waits for them, and re-layouts  0.78 us
  transfers between devices with their start and end apart: 8, of which 2 were waited for; matrix products, arithmetic and copies ran while one was open for 8% of the time, Pallas kernels for 21%

profile of v7, /device:TPU:0, one launch (start us, length us, event | category | flops | bytes accessed | tf_op | source)
XLA Modules:
  0.0 23.5 jit_solution(16027302321204133226)
XLA Ops:
  0.0 0.0 copy-start
  0.0 0.5 %collective-permute-start.1 = (bf16[64,2,4096]{2,1,0:T(2,128)(2,1)}, bf16[64,2,4096]{2,1,0:T(2,128)(2,1)S(1)}, u32[]{:S(2)}, u32[]{:S(2)}) collective-permute-start(bf16[64,2,4096]{2,1,0:T(2,128)(2,1)} %param.5), channel_id=1, source_target_pairs={{0,2},{1,3},{2,0},{3,1},{4,6},{5,7},{6,4},{7,5},{8,10},{9,11},{10,... | collective-permute-start | bytes 3145736 | tf_op jit(solution)/shard_map/ppermute | solution.py:206
  0.5 0.8 %fusion.7 = (s32[1,2,64]{2,1,0:T(2,128)S(1)}, s32[1,2,64]{2,1,0:T(2,128)S(1)}, s32[1,2,64]{2,1,0:T(2,128)S(1)}, s32[1,2,64]{2,1,0:T(2,128)S(1)}) fusion(s32[]{:T(128)S(6)} %select_n.48, s32[1,1024]{1,0:T(1,128)} %param.7, s32[1,1024]{1,0:T(1,128)} %param.6, s32[]{:T(128)S(6)} %select_n.50, s32[]{:T(128)S(6)} %select_n.52, s32[]{:T(128)S(6)} %select_n.54), kind=kLoop, calls=%fused_computation.28 | loop fusion | flops 512 | bytes 10256 | tf_op jit(solution)/shard_map/stack | solution.py:235
  1.4 0.1 add_add_fusion
  1.5 5.7 %collective-permute-start.2 = (s32[2,4,128]{2,1,0:T(4,128)S(1)}, s32[2,4,128]{2,1,0:T(4,128)S(1)}, u32[]{:S(2)}, u32[]{:S(2)}) collective-permute-start(s32[2,4,128]{2,1,0:T(4,128)S(1)} %slice.31), channel_id=1, source_target_pairs={{0,30},{1,31},{2,28},{3,29},{4,2},{5,3},{6,0},{7,1},{8,6},{9,7},{1... | collective-permute-start | bytes 12296 | tf_op jit(solution)/shard_map/ppermute | solution.py:206
  7.2 0.1 add_bitcast_fusion
  7.3 0.1 collective-permute-start
  7.4 0.8 %copy.12 = f32[16,8]{1,0:T(8,128)S(1)} copy(f32[16,8]{0,1:T(8,128)} %param.9) | data formatting | bytes 1024 | tf_op args[4]
  8.2 0.0 collective-permute-done.1
  8.2 0.2 spread.1.refs_4_
  8.4 0.2 collective-permute-done.2
  8.5 0.1 broadcast_in_dim.2.refs_2_
  8.6 0.0 copy-done
  8.6 0.0 copy-start.1
  8.6 1.7 %profiles.2 = (bf16[256,256]{1,0:T(8,128)(2,1)S(1)}, bf16[256,256]{1,0:T(8,128)(2,1)S(1)}) custom-call(s32[4,128]{1,0:T(4,128)S(1)} %get-tuple-element.41.refs_0_, s32[4,128]{1,0:T(4,128)S(1)} %get-tuple-element.40.refs_1_, f32[16,8,128]{2,1,0:T(8,128)S(1)} %broadcast_in_dim.2.refs_2_, bf16[4096,128]{1,0:T(8,128)(2,1)S(1)} %bitcast.30, ...), custom_call_target="tpu_custom_call" | custom-call | flops 1 | bytes 1 | tf_op jit(solution)/shard_map/profiles/pallas_call | solution.py:248
  10.3 0.0 collective-permute-done.refs_0_
  10.3 0.5 %collective-permute-start.7 = (bf16[256,256]{1,0:T(8,128)(2,1)S(1)}, bf16[256,256]{1,0:T(8,128)(2,1)S(1)}, u32[]{:S(2)}, u32[]{:S(2)}) collective-permute-start(bf16[256,256]{1,0:T(8,128)(2,1)S(1)} %get-tuple-element.30), channel_id=1, source_target_pairs={{0,7},{1,6},{2,5},{3,4},{4,11},{5,10},{6,9},{7,8},{8,15},{9,14},{1... | collective-permute-start | bytes 393224 | tf_op jit(solution)/shard_map/ppermute | solution.py:206
  10.9 3.1 %collective-permute-start.4 = (bf16[256,256]{1,0:T(8,128)(2,1)S(1)}, bf16[256,256]{1,0:T(8,128)(2,1)S(1)}, u32[]{:S(2)}, u32[]{:S(2)}) collective-permute-start(bf16[256,256]{1,0:T(8,128)(2,1)S(1)} %get-tuple-element.27), channel_id=1, source_target_pairs={{0,6},{1,7},{2,4},{3,5},{4,10},{5,11},{6,8},{7,9},{8,14},{9,15},{1... | collective-permute-start | bytes 393224 | tf_op jit(solution)/shard_map/ppermute | solution.py:206
  13.9 1.7 %profiles.3 = (bf16[256,128]{1,0:T(8,128)(2,1)S(1)}, bf16[256,128]{1,0:T(8,128)(2,1)S(1)}, bf16[256,128]{1,0:T(8,128)(2,1)S(1)}, bf16[256,128]{1,0:T(8,128)(2,1)S(1)}) custom-call(s32[4,128]{1,0:T(4,128)S(1)} %collective-permute-done.refs_0_, s32[4,128]{1,0:T(4,128)S(1)} %get-tuple-element.34.refs_1_, f32[16,8,128]{2,1,0:T(8,128)S(1)} %broadcast_in_dim.2.refs_2_, ...), custom_call_target="tpu_custom_call" | custom-call | flops 1 | bytes 1 | tf_op jit(solution)/shard_map/profiles/pallas_call | solution.py:248
  15.6 0.1 collective-permute-start.5
  15.7 0.1 collective-permute-start.6
  15.7 0.6 %collective-permute-start.3 = (bf16[256,128]{1,0:T(8,128)(2,1)S(1)}, bf16[256,128]{1,0:T(8,128)(2,1)S(1)}, u32[]{:S(2)}, u32[]{:S(2)}) collective-permute-start(bf16[256,128]{1,0:T(8,128)(2,1)S(1)} %get-tuple-element.26), channel_id=1, source_target_pairs={{0,1},{1,0},{2,3},{3,2},{4,5},{5,4},{6,7},{7,6},{8,9},{9,8},{10,11... | collective-permute-start | bytes 196616 | tf_op jit(solution)/shard_map/ppermute | solution.py:206
  16.4 0.0 copy-done.1
  16.4 1.1 %steering_table.1.refs_3_ = bf16[1024,512]{1,0:T(8,128)(2,1)S(1)} custom-call(f32[2,2048]{1,0:T(2,128)S(1)} %bitcast.34), custom_call_target="tpu_custom_call" | custom-call | flops 1 | bytes 1 | tf_op jit(solution)/shard_map/steering_table/pallas_call | solution.py:275
  17.4 4.6 %collective-permute-done.5.refs_0_ = bf16[256,128]{1,0:T(8,128)(2,1)S(1)} collective-permute-done((bf16[256,128]{1,0:T(8,128)(2,1)S(1)}, bf16[256,128]{1,0:T(8,128)(2,1)S(1)}, u32[]{:S(2)}, u32[]{:S(2)}) %collective-permute-start.5) | collective-permute-done | bytes 65568 | tf_op jit(solution)/shard_map/ppermute | solution.py:206
  22.1 0.0 collective-permute-done.6.refs_1_
  22.1 0.0 collective-permute-done.7.refs_2_
  22.1 0.3 %project.1.refs_4_ = f32[256,512]{1,0:T(8,128)S(1)} custom-call(bf16[256,128]{1,0:T(8,128)(2,1)S(1)} %collective-permute-done.5.refs_0_, bf16[256,128]{1,0:T(8,128)(2,1)S(1)} %collective-permute-done.6.refs_1_, bf16[256,256]{1,0:T(8,128)(2,1)S(1)} %collective-permute-done.7.refs_2_, bf16[1024,512]{1,0:T(8,128)(2,1)S(1)} %steering_table.1.refs_3_), custom_call_target="tpu_custom_call" | custom-call | flops 1 | bytes 1 | tf_op jit(solution)/shard_map/project/pallas_call | solution.py:287
  22.4 0.0 collective-permute-done.3.refs_1_
  22.4 0.0 collective-permute-done.4.refs_2_
  22.4 1.1 %finish.1 = f32[2,256,256]{2,1,0:T(8,128)} custom-call(bf16[256,128]{1,0:T(8,128)(2,1)S(1)} %get-tuple-element.25.refs_0_, bf16[256,128]{1,0:T(8,128)(2,1)S(1)} %collective-permute-done.3.refs_1_, bf16[256,256]{1,0:T(8,128)(2,1)S(1)} %collective-permute-done.4.refs_2_, bf16[1024,512]{1,0:T(8,128)(2,1)S(1)} %steering_table.1.refs_3_, ...), custom_call_target="tpu_custom_call" | custom-call | flops 1 | bytes 1 | tf_op jit(solution)/shard_map/finish/pallas_call | solution.py:298
  (8 shorter events, 0.1 us)
Async XLA Ops:
  0.0 8.6 %copy-start = (bf16[64,2,4096]{2,1,0:T(2,128)(2,1)S(1)}, bf16[64,2,4096]{2,1,0:T(2,128)(2,1)}, u32[]{:S(2)}) copy-start(bf16[64,2,4096]{2,1,0:T(2,128)(2,1)} %param.5) | copy-start | bytes 3145732
  0.0 8.2 %collective-permute-start.1 = (bf16[64,2,4096]{2,1,0:T(2,128)(2,1)}, bf16[64,2,4096]{2,1,0:T(2,128)(2,1)S(1)}, u32[]{:S(2)}, u32[]{:S(2)}) collective-permute-start(bf16[64,2,4096]{2,1,0:T(2,128)(2,1)} %param.5), channel_id=1, source_target_pairs={{0,2},{1,3},{2,0},{3,1},{4,6},{5,7},{6,4},{7,5},{8,10},{9,11},{10,... | collective-permute-start | bytes 3145736 | tf_op jit(solution)/shard_map/ppermute | solution.py:206
  1.5 7.1 %collective-permute-start.2 = (s32[2,4,128]{2,1,0:T(4,128)S(1)}, s32[2,4,128]{2,1,0:T(4,128)S(1)}, u32[]{:S(2)}, u32[]{:S(2)}) collective-permute-start(s32[2,4,128]{2,1,0:T(4,128)S(1)} %slice.31), channel_id=1, source_target_pairs={{0,30},{1,31},{2,28},{3,29},{4,2},{5,3},{6,0},{7,1},{8,6},{9,7},{1... | collective-permute-start | bytes 12296 | tf_op jit(solution)/shard_map/ppermute | solution.py:206
  7.3 3.0 %collective-permute-start = (s32[4,128]{1,0:T(4,128)S(1)}, s32[4,128]{1,0:T(4,128)S(1)}, u32[]{:S(2)}, u32[]{:S(2)}) collective-permute-start(s32[4,128]{1,0:T(4,128)S(1)} %get-tuple-element.35), channel_id=1, source_target_pairs={{0,26},{1,27},{2,0},{3,1},{4,30},{5,31},{6,4},{7,5},{8,2},{9,3},{1... | collective-permute-start | bytes 6152 | tf_op jit(solution)/shard_map/ppermute | solution.py:206
  8.6 7.7 %copy-start.1 = (f32[2,1,2048]{2,1,0:T(1,128)S(1)}, f32[2,1,2048]{2,1,0:T(1,128)}, u32[]{:S(2)}) copy-start(f32[2,1,2048]{2,1,0:T(1,128)} %param.8) | copy-start | bytes 49156
  10.3 11.7 %collective-permute-start.7 = (bf16[256,256]{1,0:T(8,128)(2,1)S(1)}, bf16[256,256]{1,0:T(8,128)(2,1)S(1)}, u32[]{:S(2)}, u32[]{:S(2)}) collective-permute-start(bf16[256,256]{1,0:T(8,128)(2,1)S(1)} %get-tuple-element.30), channel_id=1, source_target_pairs={{0,7},{1,6},{2,5},{3,4},{4,11},{5,10},{6,9},{7,8},{8,15},{9,14},{1... | collective-permute-start | bytes 393224 | tf_op jit(solution)/shard_map/ppermute | solution.py:206
  10.9 11.5 %collective-permute-start.4 = (bf16[256,256]{1,0:T(8,128)(2,1)S(1)}, bf16[256,256]{1,0:T(8,128)(2,1)S(1)}, u32[]{:S(2)}, u32[]{:S(2)}) collective-permute-start(bf16[256,256]{1,0:T(8,128)(2,1)S(1)} %get-tuple-element.27), channel_id=1, source_target_pairs={{0,6},{1,7},{2,4},{3,5},{4,10},{5,11},{6,8},{7,9},{8,14},{9,15},{1... | collective-permute-start | bytes 393224 | tf_op jit(solution)/shard_map/ppermute | solution.py:206
  15.6 6.4 %collective-permute-start.5 = (bf16[256,128]{1,0:T(8,128)(2,1)S(1)}, bf16[256,128]{1,0:T(8,128)(2,1)S(1)}, u32[]{:S(2)}, u32[]{:S(2)}) collective-permute-start(bf16[256,128]{1,0:T(8,128)(2,1)S(1)} %get-tuple-element.28), channel_id=1, source_target_pairs={{0,3},{1,2},{2,9},{3,8},{4,7},{5,6},{6,13},{7,12},{8,11},{9,10},{1... | collective-permute-start | bytes 196616 | tf_op jit(solution)/shard_map/ppermute | solution.py:206
  15.7 6.4 %collective-permute-start.6 = (bf16[256,128]{1,0:T(8,128)(2,1)S(1)}, bf16[256,128]{1,0:T(8,128)(2,1)S(1)}, u32[]{:S(2)}, u32[]{:S(2)}) collective-permute-start(bf16[256,128]{1,0:T(8,128)(2,1)S(1)} %get-tuple-element.29), channel_id=1, source_target_pairs={{0,2},{1,3},{2,8},{3,9},{4,6},{5,7},{6,12},{7,13},{8,10},{9,11},{1... | collective-permute-start | bytes 196616 | tf_op jit(solution)/shard_map/ppermute | solution.py:206
  15.7 6.6 %collective-permute-start.3 = (bf16[256,128]{1,0:T(8,128)(2,1)S(1)}, bf16[256,128]{1,0:T(8,128)(2,1)S(1)}, u32[]{:S(2)}, u32[]{:S(2)}) collective-permute-start(bf16[256,128]{1,0:T(8,128)(2,1)S(1)} %get-tuple-element.26), channel_id=1, source_target_pairs={{0,1},{1,0},{2,3},{3,2},{4,5},{5,4},{6,7},{7,6},{8,9},{9,8},{10,11... | collective-permute-start | bytes 196616 | tf_op jit(solution)/shard_map/ppermute | solution.py:206
